TPU v7x, 256 devices: a whole 4x4x8 slice. The times are simulated.
256 devices in a mesh: pipe: 8 (over y_hi, x), fsdp: 32 (over y_lo, z, core).
Axes of the slice: x: 4, y: 4 (y_hi: 2, y_lo: 2; y = y_hi * 2 + y_lo), z: 8, core: 2. Of those that a mesh axis runs over, the one named last changes fastest.
Arguments:
- inputs: bfloat16 [8, 768, 4096], P(None, 'fsdp'), may hold values from -6 to 6
- gains: float32 [16, 4096], P('pipe'), may hold values from 0.25 to 1.75
- proj_gate: bfloat16 [16, 4096, 512], P('pipe', 'fsdp'), may hold values from -0.09375 to 0.09375
- proj_in: bfloat16 [16, 4096, 512], P('pipe', 'fsdp'), may hold values from -0.09375 to 0.09375
- proj_out: bfloat16 [16, 512, 4096], P('pipe', None, 'fsdp'), may hold values from -0.25 to 0.25
- plan: int32 [8], replicated, may hold values from 0 to 7, each once
Outputs:
- finished: bfloat16 [8, 768, 4096], P('pipe', 'fsdp')
Inputs may be any that keep to these rules, and one draw needn't show every extreme that they name: `plan`: each slot names a different micro-batch.
All inputs are finite; a program needn't handle non-finite values.
Results may differ from a plain program's by a relative error of at most 0.039.
Values may be sent and summed in bfloat16 or wider, within the bound.
A program may use at most 128 MiB of HBM per device.

v0:
```python
import jax
import jax.numpy as jnp
from jax import lax
from jax.sharding import PartitionSpec as P


def shifted(value, axis, by):
    count = lax.axis_size(axis)
    return lax.ppermute(value, axis, [(i, (i + by) % count) for i in range(count)])


def advance(state, gain, w_gate, w_first, w_second):
    wide = state.astype(jnp.float32)
    scale = lax.rsqrt(jnp.mean(wide * wide, axis=-1, keepdims=True) + 1e-05)
    normed = (wide * scale * gain).astype(jnp.bfloat16)
    gated = jax.nn.silu(jnp.dot(normed, w_gate, preferred_element_type=jnp.float32))
    hidden = (gated * jnp.dot(normed, w_first, preferred_element_type=jnp.float32)).astype(
        jnp.bfloat16
    )
    return (wide + jnp.dot(hidden, w_second, preferred_element_type=jnp.float32)).astype(
        jnp.bfloat16
    )


def local(inputs, gains, proj_gate, proj_in, proj_out, plan):
    sections = lax.axis_size("pipe")
    section = lax.axis_index("pipe")
    tok_rows = inputs.shape[1]
    width = inputs.shape[2]

    def locate(step):
        slot = jnp.mod(step - section, sections)
        progress = step - slot
        lap = jnp.floor_divide(progress - section, sections)
        active = (progress >= 0) & (lap < 2)
        keep = (progress >= 0) & (lap == 2) & (slot == section)
        fresh = (section == 0) & (progress == 0)
        return (slot, jnp.clip(lap, 0, 1), active, keep, fresh)

    def entering(step, carry):
        slot, lap, active, keep, fresh = locate(step)
        received = shifted(carry, "pipe", 1)
        picked = lax.dynamic_index_in_dim(plan, slot, 0, keepdims=False)
        first = lax.dynamic_index_in_dim(inputs, picked, 0, keepdims=False)
        source = jnp.where(fresh, first, received)
        gain = lax.dynamic_index_in_dim(gains, lap, 0, keepdims=False)
        return (source, lap, active, keep, gain)

    def make_step(full_gate, full_first, full_second):

        def one_step(step, state):
            carry, result = state
            source, lap, active, keep, gain = entering(step, carry)
            w_gate = lax.dynamic_index_in_dim(full_gate, lap, 0, keepdims=False)
            w_first = lax.dynamic_index_in_dim(full_first, lap, 0, keepdims=False)
            w_second = lax.dynamic_index_in_dim(full_second, lap, 0, keepdims=False)
            moved = lax.cond(
                active,
                lambda rows: advance(rows, gain, w_gate, w_first, w_second),
                lambda rows: rows,
                source,
            )
            return (moved, jnp.where(keep, source, result))

        return one_step

    blank = jnp.zeros((tok_rows, width), jnp.bfloat16)
    state = (blank, blank)
    total_steps = 4 * sections - 1
    full_gate, full_first, full_second = (
        lax.all_gather(proj_gate, "fsdp", axis=1, tiled=True),
        lax.all_gather(proj_in, "fsdp", axis=1, tiled=True),
        lax.all_gather(proj_out, "fsdp", axis=2, tiled=True),
    )
    state = lax.fori_loop(0, total_steps, make_step(full_gate, full_first, full_second), state)
    return state[1][None]


def solution(mesh):
    in_specs = (
        P(None, "fsdp", None),
        P("pipe", None),
        P("pipe", "fsdp", None),
        P("pipe", "fsdp", None),
        P("pipe", None, "fsdp"),
        P(),
    )
    out_specs = P("pipe", "fsdp", None)
    return jax.shard_map(local, mesh=mesh, in_specs=in_specs, out_specs=out_specs, check_vma=False)
```

profile of v0, /device:TPU:20, one launch (start us, length us, event | category | flops | bytes accessed | tf_op | source)
XLA Modules:
  0.0 750.2 jit_solution(5577276827017783515)
XLA Ops:
  8.8 75.6 %all-gather.4.cloned.1.call-done = bf16[2,4096,512]{2,1,0:T(8,128)(2,1)} async-done(((bf16[2,128,512]{2,1,0:T(8,128)(2,1)}), bf16[2,4096,512]{2,1,0:T(8,128)(2,1)}) %all-gather.4.cloned.1.call-update) | async-done | bytes 8388624 | tf_op jit(solution)/shard_map/all_gather | solution.py:71
  84.3 74.1 %all-gather.6.cloned.1.call-done = bf16[2,4096,512]{2,1,0:T(8,128)(2,1)} async-done(((bf16[2,128,512]{2,1,0:T(8,128)(2,1)}), bf16[2,4096,512]{2,1,0:T(8,128)(2,1)}) %all-gather.6.cloned.1.call-update) | async-done | bytes 8388624 | tf_op jit(solution)/shard_map/all_gather | solution.py:72
  158.4 90.6 %all-gather.8.cloned.1.call-done = bf16[2,512,4096]{2,1,0:T(8,128)(2,1)} async-done(((bf16[2,512,128]{2,1,0:T(8,128)(2,1)}), bf16[2,512,4096]{2,1,0:T(8,128)(2,1)}) %all-gather.8.cloned.1.call-update) | async-done | bytes 8388624 | tf_op jit(solution)/shard_map/all_gather | solution.py:73
  249.0 494.0 %while.18 = (s32[]{:T(128)}, bf16[24,4096]{1,0:T(8,128)(2,1)S(1)}, bf16[24,4096]{1,0:T(8,128)(2,1)S(1)}, s32[]{:T(128)}, pred[]{:T(512)}, /*index=5*/s32[8]{0:T(...) while((s32[]{:T(128)}, bf16[24,4096]{1,0:T(8,128)(2,1)S(1)}, ...), condition=%wide.region_4.5_spmd.clone, body=%wide.region_0.4_spmd.clone.sunk | while | flops 303734848 | bytes 15895146 | solution.py:75
  264.6 12.6 %collective-permute-start = (bf16[24,4096]{1,0:T(8,128)(2,1)S(1)}, bf16[24,4096]{1,0:T(8,128)(2,1)S(1)}, u32[]{:S(2)}, u32[]{:S(2)}) collective-permute-start(bf16[24,4096]{1,0:T(8,128)(2,1)S(1)} %get-tuple-element.487), channel_id=1, source_target_pairs={{0,32},{32,64},{64,96},{96,128},{128,160},{160,192},{192,224},{224... | collective-permute-start | bytes 589832 | tf_op jit(solution)/shard_map/while/body/eval_jaxpr/ppermute | solution.py:9
  281.5 14.9 %collective-permute-start = (bf16[24,4096]{1,0:T(8,128)(2,1)S(1)}, bf16[24,4096]{1,0:T(8,128)(2,1)S(1)}, u32[]{:S(2)}, u32[]{:S(2)}) collective-permute-start(bf16[24,4096]{1,0:T(8,128)(2,1)S(1)} %get-tuple-element.487), channel_id=1, source_target_pairs={{0,32},{32,64},{64,96},{96,128},{128,160},{160,192},{192,224},{224... | collective-permute-start | bytes 589832 | tf_op jit(solution)/shard_map/while/body/eval_jaxpr/ppermute | solution.py:9
  300.7 14.9 %collective-permute-start = (bf16[24,4096]{1,0:T(8,128)(2,1)S(1)}, bf16[24,4096]{1,0:T(8,128)(2,1)S(1)}, u32[]{:S(2)}, u32[]{:S(2)}) collective-permute-start(bf16[24,4096]{1,0:T(8,128)(2,1)S(1)} %get-tuple-element.487), channel_id=1, source_target_pairs={{0,32},{32,64},{64,96},{96,128},{128,160},{160,192},{192,224},{224... | collective-permute-start | bytes 589832 | tf_op jit(solution)/shard_map/while/body/eval_jaxpr/ppermute | solution.py:9
  319.8 14.9 %collective-permute-start = (bf16[24,4096]{1,0:T(8,128)(2,1)S(1)}, bf16[24,4096]{1,0:T(8,128)(2,1)S(1)}, u32[]{:S(2)}, u32[]{:S(2)}) collective-permute-start(bf16[24,4096]{1,0:T(8,128)(2,1)S(1)} %get-tuple-element.487), channel_id=1, source_target_pairs={{0,32},{32,64},{64,96},{96,128},{128,160},{160,192},{192,224},{224... | collective-permute-start | bytes 589832 | tf_op jit(solution)/shard_map/while/body/eval_jaxpr/ppermute | solution.py:9
  339.0 14.9 %collective-permute-start = (bf16[24,4096]{1,0:T(8,128)(2,1)S(1)}, bf16[24,4096]{1,0:T(8,128)(2,1)S(1)}, u32[]{:S(2)}, u32[]{:S(2)}) collective-permute-start(bf16[24,4096]{1,0:T(8,128)(2,1)S(1)} %get-tuple-element.487), channel_id=1, source_target_pairs={{0,32},{32,64},{64,96},{96,128},{128,160},{160,192},{192,224},{224... | collective-permute-start | bytes 589832 | tf_op jit(solution)/shard_map/while/body/eval_jaxpr/ppermute | solution.py:9
  358.1 8.7 %conditional.3 = (bf16[24,4096]{1,0:T(8,128)(2,1)S(1)}) conditional(s32[]{:T(128)} %convert_element_type.52, bf16[24,4096]{1,0:T(8,128)(2,1)S(1)} %get-tuple-element.466, (bf16[24,4096]{1,0:T(8,128)(2,1)S(1)}, s32[]{:T(128)}, f32[2,4096]{1,0:T(2,128)}, bf16[2,4096,512]{2,1,0:T(8,128)(2,1)}, bf16[2,4096,512]{2,1,0:T(8,128)(2,1)}, ...), branch_computations={%region_1.1_spmd, %region_2.3_spmd} | conditional | flops 303439904 | bytes 14124968 | solution.py:57
  362.0 4.8 fusion
  366.8 6.2 collective-permute-start
  377.2 8.7 %conditional.3 = (bf16[24,4096]{1,0:T(8,128)(2,1)S(1)}) conditional(s32[]{:T(128)} %convert_element_type.52, bf16[24,4096]{1,0:T(8,128)(2,1)S(1)} %get-tuple-element.466, (bf16[24,4096]{1,0:T(8,128)(2,1)S(1)}, s32[]{:T(128)}, f32[2,4096]{1,0:T(2,128)}, bf16[2,4096,512]{2,1,0:T(8,128)(2,1)}, bf16[2,4096,512]{2,1,0:T(8,128)(2,1)}, ...), branch_computations={%region_1.1_spmd, %region_2.3_spmd} | conditional | flops 303439904 | bytes 14124968 | solution.py:57
  378.2 2.9 fusion.4
  381.1 4.8 fusion
  386.0 14.9 %collective-permute-start = (bf16[24,4096]{1,0:T(8,128)(2,1)S(1)}, bf16[24,4096]{1,0:T(8,128)(2,1)S(1)}, u32[]{:S(2)}, u32[]{:S(2)}) collective-permute-start(bf16[24,4096]{1,0:T(8,128)(2,1)S(1)} %get-tuple-element.487), channel_id=1, source_target_pairs={{0,32},{32,64},{64,96},{96,128},{128,160},{160,192},{192,224},{224... | collective-permute-start | bytes 589832 | tf_op jit(solution)/shard_map/while/body/eval_jaxpr/ppermute | solution.py:9
  405.1 8.7 %conditional.3 = (bf16[24,4096]{1,0:T(8,128)(2,1)S(1)}) conditional(s32[]{:T(128)} %convert_element_type.52, bf16[24,4096]{1,0:T(8,128)(2,1)S(1)} %get-tuple-element.466, (bf16[24,4096]{1,0:T(8,128)(2,1)S(1)}, s32[]{:T(128)}, f32[2,4096]{1,0:T(2,128)}, bf16[2,4096,512]{2,1,0:T(8,128)(2,1)}, bf16[2,4096,512]{2,1,0:T(8,128)(2,1)}, ...), branch_computations={%region_1.1_spmd, %region_2.3_spmd} | conditional | flops 303439904 | bytes 14124968 | solution.py:57
  409.0 4.8 fusion
  413.9 6.2 collective-permute-start
  424.2 8.7 %conditional.3 = (bf16[24,4096]{1,0:T(8,128)(2,1)S(1)}) conditional(s32[]{:T(128)} %convert_element_type.52, bf16[24,4096]{1,0:T(8,128)(2,1)S(1)} %get-tuple-element.466, (bf16[24,4096]{1,0:T(8,128)(2,1)S(1)}, s32[]{:T(128)}, f32[2,4096]{1,0:T(2,128)}, bf16[2,4096,512]{2,1,0:T(8,128)(2,1)}, bf16[2,4096,512]{2,1,0:T(8,128)(2,1)}, ...), branch_computations={%region_1.1_spmd, %region_2.3_spmd} | conditional | flops 303439904 | bytes 14124968 | solution.py:57
  425.2 2.9 fusion.4
  428.1 4.8 fusion
  433.0 6.2 collective-permute-start
  443.4 8.7 %conditional.3 = (bf16[24,4096]{1,0:T(8,128)(2,1)S(1)}) conditional(s32[]{:T(128)} %convert_element_type.52, bf16[24,4096]{1,0:T(8,128)(2,1)S(1)} %get-tuple-element.466, (bf16[24,4096]{1,0:T(8,128)(2,1)S(1)}, s32[]{:T(128)}, f32[2,4096]{1,0:T(2,128)}, bf16[2,4096,512]{2,1,0:T(8,128)(2,1)}, bf16[2,4096,512]{2,1,0:T(8,128)(2,1)}, ...), branch_computations={%region_1.1_spmd, %region_2.3_spmd} | conditional | flops 303439904 | bytes 14124968 | solution.py:57
  447.3 4.8 fusion
  452.1 6.2 collective-permute-start
  462.5 8.7 %conditional.3 = (bf16[24,4096]{1,0:T(8,128)(2,1)S(1)}) conditional(s32[]{:T(128)} %convert_element_type.52, bf16[24,4096]{1,0:T(8,128)(2,1)S(1)} %get-tuple-element.466, (bf16[24,4096]{1,0:T(8,128)(2,1)S(1)}, s32[]{:T(128)}, f32[2,4096]{1,0:T(2,128)}, bf16[2,4096,512]{2,1,0:T(8,128)(2,1)}, bf16[2,4096,512]{2,1,0:T(8,128)(2,1)}, ...), branch_computations={%region_1.1_spmd, %region_2.3_spmd} | conditional | flops 303439904 | bytes 14124968 | solution.py:57
  463.5 2.9 fusion.4
  466.4 4.8 fusion
  471.3 6.2 collective-permute-start
  481.7 8.7 %conditional.3 = (bf16[24,4096]{1,0:T(8,128)(2,1)S(1)}) conditional(s32[]{:T(128)} %convert_element_type.52, bf16[24,4096]{1,0:T(8,128)(2,1)S(1)} %get-tuple-element.466, (bf16[24,4096]{1,0:T(8,128)(2,1)S(1)}, s32[]{:T(128)}, f32[2,4096]{1,0:T(2,128)}, bf16[2,4096,512]{2,1,0:T(8,128)(2,1)}, bf16[2,4096,512]{2,1,0:T(8,128)(2,1)}, ...), branch_computations={%region_1.1_spmd, %region_2.3_spmd} | conditional | flops 303439904 | bytes 14124968 | solution.py:57
  482.7 2.9 fusion.4
  485.6 4.8 fusion
  490.4 6.2 collective-permute-start
  500.8 8.7 %conditional.3 = (bf16[24,4096]{1,0:T(8,128)(2,1)S(1)}) conditional(s32[]{:T(128)} %convert_element_type.52, bf16[24,4096]{1,0:T(8,128)(2,1)S(1)} %get-tuple-element.466, (bf16[24,4096]{1,0:T(8,128)(2,1)S(1)}, s32[]{:T(128)}, f32[2,4096]{1,0:T(2,128)}, bf16[2,4096,512]{2,1,0:T(8,128)(2,1)}, bf16[2,4096,512]{2,1,0:T(8,128)(2,1)}, ...), branch_computations={%region_1.1_spmd, %region_2.3_spmd} | conditional | flops 303439904 | bytes 14124968 | solution.py:57
  504.7 4.8 fusion
  509.6 6.2 collective-permute-start
  520.0 8.7 %conditional.3 = (bf16[24,4096]{1,0:T(8,128)(2,1)S(1)}) conditional(s32[]{:T(128)} %convert_element_type.52, bf16[24,4096]{1,0:T(8,128)(2,1)S(1)} %get-tuple-element.466, (bf16[24,4096]{1,0:T(8,128)(2,1)S(1)}, s32[]{:T(128)}, f32[2,4096]{1,0:T(2,128)}, bf16[2,4096,512]{2,1,0:T(8,128)(2,1)}, bf16[2,4096,512]{2,1,0:T(8,128)(2,1)}, ...), branch_computations={%region_1.1_spmd, %region_2.3_spmd} | conditional | flops 303439904 | bytes 14124968 | solution.py:57
  521.0 2.9 fusion.4
  523.9 4.8 fusion
  528.7 6.4 collective-permute-start
  540.3 8.7 %conditional.3 = (bf16[24,4096]{1,0:T(8,128)(2,1)S(1)}) conditional(s32[]{:T(128)} %convert_element_type.52, bf16[24,4096]{1,0:T(8,128)(2,1)S(1)} %get-tuple-element.466, (bf16[24,4096]{1,0:T(8,128)(2,1)S(1)}, s32[]{:T(128)}, f32[2,4096]{1,0:T(2,128)}, bf16[2,4096,512]{2,1,0:T(8,128)(2,1)}, bf16[2,4096,512]{2,1,0:T(8,128)(2,1)}, ...), branch_computations={%region_1.1_spmd, %region_2.3_spmd} | conditional | flops 303439904 | bytes 14124968 | solution.py:57
  544.2 4.8 fusion
  549.0 6.8 collective-permute-start
  561.9 8.7 %conditional.3 = (bf16[24,4096]{1,0:T(8,128)(2,1)S(1)}) conditional(s32[]{:T(128)} %convert_element_type.52, bf16[24,4096]{1,0:T(8,128)(2,1)S(1)} %get-tuple-element.466, (bf16[24,4096]{1,0:T(8,128)(2,1)S(1)}, s32[]{:T(128)}, f32[2,4096]{1,0:T(2,128)}, bf16[2,4096,512]{2,1,0:T(8,128)(2,1)}, bf16[2,4096,512]{2,1,0:T(8,128)(2,1)}, ...), branch_computations={%region_1.1_spmd, %region_2.3_spmd} | conditional | flops 303439904 | bytes 14124968 | solution.py:57
  565.8 4.8 fusion
  570.6 4.3 collective-permute-start
  579.2 8.7 %conditional.3 = (bf16[24,4096]{1,0:T(8,128)(2,1)S(1)}) conditional(s32[]{:T(128)} %convert_element_type.52, bf16[24,4096]{1,0:T(8,128)(2,1)S(1)} %get-tuple-element.466, (bf16[24,4096]{1,0:T(8,128)(2,1)S(1)}, s32[]{:T(128)}, f32[2,4096]{1,0:T(2,128)}, bf16[2,4096,512]{2,1,0:T(8,128)(2,1)}, bf16[2,4096,512]{2,1,0:T(8,128)(2,1)}, ...), branch_computations={%region_1.1_spmd, %region_2.3_spmd} | conditional | flops 303439904 | bytes 14124968 | solution.py:57
  583.1 4.8 fusion
  594.7 8.7 %conditional.3 = (bf16[24,4096]{1,0:T(8,128)(2,1)S(1)}) conditional(s32[]{:T(128)} %convert_element_type.52, bf16[24,4096]{1,0:T(8,128)(2,1)S(1)} %get-tuple-element.466, (bf16[24,4096]{1,0:T(8,128)(2,1)S(1)}, s32[]{:T(128)}, f32[2,4096]{1,0:T(2,128)}, bf16[2,4096,512]{2,1,0:T(8,128)(2,1)}, bf16[2,4096,512]{2,1,0:T(8,128)(2,1)}, ...), branch_computations={%region_1.1_spmd, %region_2.3_spmd} | conditional | flops 303439904 | bytes 14124968 | solution.py:57
  598.6 4.8 fusion
  610.3 8.7 %conditional.3 = (bf16[24,4096]{1,0:T(8,128)(2,1)S(1)}) conditional(s32[]{:T(128)} %convert_element_type.52, bf16[24,4096]{1,0:T(8,128)(2,1)S(1)} %get-tuple-element.466, (bf16[24,4096]{1,0:T(8,128)(2,1)S(1)}, s32[]{:T(128)}, f32[2,4096]{1,0:T(2,128)}, bf16[2,4096,512]{2,1,0:T(8,128)(2,1)}, bf16[2,4096,512]{2,1,0:T(8,128)(2,1)}, ...), branch_computations={%region_1.1_spmd, %region_2.3_spmd} | conditional | flops 303439904 | bytes 14124968 | solution.py:57
  614.2 4.8 fusion
  625.8 8.7 %conditional.3 = (bf16[24,4096]{1,0:T(8,128)(2,1)S(1)}) conditional(s32[]{:T(128)} %convert_element_type.52, bf16[24,4096]{1,0:T(8,128)(2,1)S(1)} %get-tuple-element.466, (bf16[24,4096]{1,0:T(8,128)(2,1)S(1)}, s32[]{:T(128)}, f32[2,4096]{1,0:T(2,128)}, bf16[2,4096,512]{2,1,0:T(8,128)(2,1)}, bf16[2,4096,512]{2,1,0:T(8,128)(2,1)}, ...), branch_computations={%region_1.1_spmd, %region_2.3_spmd} | conditional | flops 303439904 | bytes 14124968 | solution.py:57
  629.7 4.8 fusion
  640.3 3.1 collective-permute-done
  644.4 8.7 %conditional.3 = (bf16[24,4096]{1,0:T(8,128)(2,1)S(1)}) conditional(s32[]{:T(128)} %convert_element_type.52, bf16[24,4096]{1,0:T(8,128)(2,1)S(1)} %get-tuple-element.466, (bf16[24,4096]{1,0:T(8,128)(2,1)S(1)}, s32[]{:T(128)}, f32[2,4096]{1,0:T(2,128)}, bf16[2,4096,512]{2,1,0:T(8,128)(2,1)}, bf16[2,4096,512]{2,1,0:T(8,128)(2,1)}, ...), branch_computations={%region_1.1_spmd, %region_2.3_spmd} | conditional | flops 303439904 | bytes 14124968 | solution.py:57
  648.3 4.8 fusion
  656.5 4.0 collective-permute-done
  661.6 7.2 collective-permute-start
  700.1 5.3 collective-permute-start
  711.5 6.3 collective-permute-start
  722.1 6.2 collective-permute-start
  732.6 6.2 collective-permute-start
  (201 shorter events, 157.7 us)
Async XLA Ops:
  6.5 77.8 %all-gather.4.cloned.1.call-start = ((), (), s32[]{:S(2)}) async-start(), calls=%async_computation | async-start | bytes 8650752 | tf_op jit(solution)/shard_map/all_gather | solution.py:71
  7.3 151.2 %all-gather.6.cloned.1.call-start = ((), (), s32[]{:S(2)}) async-start(), calls=%async_computation.1 | async-start | bytes 8650752 | tf_op jit(solution)/shard_map/all_gather | solution.py:72
  8.0 241.0 %all-gather.8.cloned.1.call-start = ((), (), s32[]{:S(2)}) async-start(), calls=%async_computation.2 | async-start | bytes 8650752 | tf_op jit(solution)/shard_map/all_gather | solution.py:73
  249.0 7.1 collective-permute-start
  257.2 6.3 collective-permute-start
  264.6 15.8 %collective-permute-start = (bf16[24,4096]{1,0:T(8,128)(2,1)S(1)}, bf16[24,4096]{1,0:T(8,128)(2,1)S(1)}, u32[]{:S(2)}, u32[]{:S(2)}) collective-permute-start(bf16[24,4096]{1,0:T(8,128)(2,1)S(1)} %get-tuple-element.487), channel_id=1, source_target_pairs={{0,32},{32,64},{64,96},{96,128},{128,160},{160,192},{192,224},{224... | collective-permute-start | bytes 589832 | tf_op jit(solution)/shard_map/while/body/eval_jaxpr/ppermute | solution.py:9
  281.5 18.1 %collective-permute-start = (bf16[24,4096]{1,0:T(8,128)(2,1)S(1)}, bf16[24,4096]{1,0:T(8,128)(2,1)S(1)}, u32[]{:S(2)}, u32[]{:S(2)}) collective-permute-start(bf16[24,4096]{1,0:T(8,128)(2,1)S(1)} %get-tuple-element.487), channel_id=1, source_target_pairs={{0,32},{32,64},{64,96},{96,128},{128,160},{160,192},{192,224},{224... | collective-permute-start | bytes 589832 | tf_op jit(solution)/shard_map/while/body/eval_jaxpr/ppermute | solution.py:9
  300.7 18.1 %collective-permute-start = (bf16[24,4096]{1,0:T(8,128)(2,1)S(1)}, bf16[24,4096]{1,0:T(8,128)(2,1)S(1)}, u32[]{:S(2)}, u32[]{:S(2)}) collective-permute-start(bf16[24,4096]{1,0:T(8,128)(2,1)S(1)} %get-tuple-element.487), channel_id=1, source_target_pairs={{0,32},{32,64},{64,96},{96,128},{128,160},{160,192},{192,224},{224... | collective-permute-start | bytes 589832 | tf_op jit(solution)/shard_map/while/body/eval_jaxpr/ppermute | solution.py:9
  319.8 18.1 %collective-permute-start = (bf16[24,4096]{1,0:T(8,128)(2,1)S(1)}, bf16[24,4096]{1,0:T(8,128)(2,1)S(1)}, u32[]{:S(2)}, u32[]{:S(2)}) collective-permute-start(bf16[24,4096]{1,0:T(8,128)(2,1)S(1)} %get-tuple-element.487), channel_id=1, source_target_pairs={{0,32},{32,64},{64,96},{96,128},{128,160},{160,192},{192,224},{224... | collective-permute-start | bytes 589832 | tf_op jit(solution)/shard_map/while/body/eval_jaxpr/ppermute | solution.py:9
  339.0 18.1 %collective-permute-start = (bf16[24,4096]{1,0:T(8,128)(2,1)S(1)}, bf16[24,4096]{1,0:T(8,128)(2,1)S(1)}, u32[]{:S(2)}, u32[]{:S(2)}) collective-permute-start(bf16[24,4096]{1,0:T(8,128)(2,1)S(1)} %get-tuple-element.487), channel_id=1, source_target_pairs={{0,32},{32,64},{64,96},{96,128},{128,160},{160,192},{192,224},{224... | collective-permute-start | bytes 589832 | tf_op jit(solution)/shard_map/while/body/eval_jaxpr/ppermute | solution.py:9
  366.8 9.3 %collective-permute-start = (bf16[24,4096]{1,0:T(8,128)(2,1)S(1)}, bf16[24,4096]{1,0:T(8,128)(2,1)S(1)}, u32[]{:S(2)}, u32[]{:S(2)}) collective-permute-start(bf16[24,4096]{1,0:T(8,128)(2,1)S(1)} %get-tuple-element.487), channel_id=1, source_target_pairs={{0,32},{32,64},{64,96},{96,128},{128,160},{160,192},{192,224},{224... | collective-permute-start | bytes 589832 | tf_op jit(solution)/shard_map/while/body/eval_jaxpr/ppermute | solution.py:9
  386.0 18.1 %collective-permute-start = (bf16[24,4096]{1,0:T(8,128)(2,1)S(1)}, bf16[24,4096]{1,0:T(8,128)(2,1)S(1)}, u32[]{:S(2)}, u32[]{:S(2)}) collective-permute-start(bf16[24,4096]{1,0:T(8,128)(2,1)S(1)} %get-tuple-element.487), channel_id=1, source_target_pairs={{0,32},{32,64},{64,96},{96,128},{128,160},{160,192},{192,224},{224... | collective-permute-start | bytes 589832 | tf_op jit(solution)/shard_map/while/body/eval_jaxpr/ppermute | solution.py:9
  413.9 9.3 %collective-permute-start = (bf16[24,4096]{1,0:T(8,128)(2,1)S(1)}, bf16[24,4096]{1,0:T(8,128)(2,1)S(1)}, u32[]{:S(2)}, u32[]{:S(2)}) collective-permute-start(bf16[24,4096]{1,0:T(8,128)(2,1)S(1)} %get-tuple-element.487), channel_id=1, source_target_pairs={{0,32},{32,64},{64,96},{96,128},{128,160},{160,192},{192,224},{224... | collective-permute-start | bytes 589832 | tf_op jit(solution)/shard_map/while/body/eval_jaxpr/ppermute | solution.py:9
  433.0 9.3 %collective-permute-start = (bf16[24,4096]{1,0:T(8,128)(2,1)S(1)}, bf16[24,4096]{1,0:T(8,128)(2,1)S(1)}, u32[]{:S(2)}, u32[]{:S(2)}) collective-permute-start(bf16[24,4096]{1,0:T(8,128)(2,1)S(1)} %get-tuple-element.487), channel_id=1, source_target_pairs={{0,32},{32,64},{64,96},{96,128},{128,160},{160,192},{192,224},{224... | collective-permute-start | bytes 589832 | tf_op jit(solution)/shard_map/while/body/eval_jaxpr/ppermute | solution.py:9
  452.1 9.3 %collective-permute-start = (bf16[24,4096]{1,0:T(8,128)(2,1)S(1)}, bf16[24,4096]{1,0:T(8,128)(2,1)S(1)}, u32[]{:S(2)}, u32[]{:S(2)}) collective-permute-start(bf16[24,4096]{1,0:T(8,128)(2,1)S(1)} %get-tuple-element.487), channel_id=1, source_target_pairs={{0,32},{32,64},{64,96},{96,128},{128,160},{160,192},{192,224},{224... | collective-permute-start | bytes 589832 | tf_op jit(solution)/shard_map/while/body/eval_jaxpr/ppermute | solution.py:9
  471.3 9.3 %collective-permute-start = (bf16[24,4096]{1,0:T(8,128)(2,1)S(1)}, bf16[24,4096]{1,0:T(8,128)(2,1)S(1)}, u32[]{:S(2)}, u32[]{:S(2)}) collective-permute-start(bf16[24,4096]{1,0:T(8,128)(2,1)S(1)} %get-tuple-element.487), channel_id=1, source_target_pairs={{0,32},{32,64},{64,96},{96,128},{128,160},{160,192},{192,224},{224... | collective-permute-start | bytes 589832 | tf_op jit(solution)/shard_map/while/body/eval_jaxpr/ppermute | solution.py:9
  490.4 9.3 %collective-permute-start = (bf16[24,4096]{1,0:T(8,128)(2,1)S(1)}, bf16[24,4096]{1,0:T(8,128)(2,1)S(1)}, u32[]{:S(2)}, u32[]{:S(2)}) collective-permute-start(bf16[24,4096]{1,0:T(8,128)(2,1)S(1)} %get-tuple-element.487), channel_id=1, source_target_pairs={{0,32},{32,64},{64,96},{96,128},{128,160},{160,192},{192,224},{224... | collective-permute-start | bytes 589832 | tf_op jit(solution)/shard_map/while/body/eval_jaxpr/ppermute | solution.py:9
  509.6 9.3 %collective-permute-start = (bf16[24,4096]{1,0:T(8,128)(2,1)S(1)}, bf16[24,4096]{1,0:T(8,128)(2,1)S(1)}, u32[]{:S(2)}, u32[]{:S(2)}) collective-permute-start(bf16[24,4096]{1,0:T(8,128)(2,1)S(1)} %get-tuple-element.487), channel_id=1, source_target_pairs={{0,32},{32,64},{64,96},{96,128},{128,160},{160,192},{192,224},{224... | collective-permute-start | bytes 589832 | tf_op jit(solution)/shard_map/while/body/eval_jaxpr/ppermute | solution.py:9
  528.7 10.5 %collective-permute-start = (bf16[24,4096]{1,0:T(8,128)(2,1)S(1)}, bf16[24,4096]{1,0:T(8,128)(2,1)S(1)}, u32[]{:S(2)}, u32[]{:S(2)}) collective-permute-start(bf16[24,4096]{1,0:T(8,128)(2,1)S(1)} %get-tuple-element.487), channel_id=1, source_target_pairs={{0,32},{32,64},{64,96},{96,128},{128,160},{160,192},{192,224},{224... | collective-permute-start | bytes 589832 | tf_op jit(solution)/shard_map/while/body/eval_jaxpr/ppermute | solution.py:9
  549.0 11.8 %collective-permute-start = (bf16[24,4096]{1,0:T(8,128)(2,1)S(1)}, bf16[24,4096]{1,0:T(8,128)(2,1)S(1)}, u32[]{:S(2)}, u32[]{:S(2)}) collective-permute-start(bf16[24,4096]{1,0:T(8,128)(2,1)S(1)} %get-tuple-element.487), channel_id=1, source_target_pairs={{0,32},{32,64},{64,96},{96,128},{128,160},{160,192},{192,224},{224... | collective-permute-start | bytes 589832 | tf_op jit(solution)/shard_map/while/body/eval_jaxpr/ppermute | solution.py:9
  570.6 7.5 %collective-permute-start = (bf16[24,4096]{1,0:T(8,128)(2,1)S(1)}, bf16[24,4096]{1,0:T(8,128)(2,1)S(1)}, u32[]{:S(2)}, u32[]{:S(2)}) collective-permute-start(bf16[24,4096]{1,0:T(8,128)(2,1)S(1)} %get-tuple-element.487), channel_id=1, source_target_pairs={{0,32},{32,64},{64,96},{96,128},{128,160},{160,192},{192,224},{224... | collective-permute-start | bytes 589832 | tf_op jit(solution)/shard_map/while/body/eval_jaxpr/ppermute | solution.py:9
  588.0 5.7 collective-permute-start
  603.5 5.7 collective-permute-start
  619.0 5.7 collective-permute-start
  634.6 8.8 %collective-permute-start = (bf16[24,4096]{1,0:T(8,128)(2,1)S(1)}, bf16[24,4096]{1,0:T(8,128)(2,1)S(1)}, u32[]{:S(2)}, u32[]{:S(2)}) collective-permute-start(bf16[24,4096]{1,0:T(8,128)(2,1)S(1)} %get-tuple-element.487), channel_id=1, source_target_pairs={{0,32},{32,64},{64,96},{96,128},{128,160},{160,192},{192,224},{224... | collective-permute-start | bytes 589832 | tf_op jit(solution)/shard_map/while/body/eval_jaxpr/ppermute | solution.py:9
  653.1 7.4 collective-permute-start
  661.6 11.8 %collective-permute-start = (bf16[24,4096]{1,0:T(8,128)(2,1)S(1)}, bf16[24,4096]{1,0:T(8,128)(2,1)S(1)}, u32[]{:S(2)}, u32[]{:S(2)}) collective-permute-start(bf16[24,4096]{1,0:T(8,128)(2,1)S(1)} %get-tuple-element.487), channel_id=1, source_target_pairs={{0,32},{32,64},{64,96},{96,128},{128,160},{160,192},{192,224},{224... | collective-permute-start | bytes 589832 | tf_op jit(solution)/shard_map/while/body/eval_jaxpr/ppermute | solution.py:9
  674.4 7.6 %collective-permute-start = (bf16[24,4096]{1,0:T(8,128)(2,1)S(1)}, bf16[24,4096]{1,0:T(8,128)(2,1)S(1)}, u32[]{:S(2)}, u32[]{:S(2)}) collective-permute-start(bf16[24,4096]{1,0:T(8,128)(2,1)S(1)} %get-tuple-element.487), channel_id=1, source_target_pairs={{0,32},{32,64},{64,96},{96,128},{128,160},{160,192},{192,224},{224... | collective-permute-start | bytes 589832 | tf_op jit(solution)/shard_map/while/body/eval_jaxpr/ppermute | solution.py:9
  683.1 7.3 collective-permute-start
  691.4 7.6 %collective-permute-start = (bf16[24,4096]{1,0:T(8,128)(2,1)S(1)}, bf16[24,4096]{1,0:T(8,128)(2,1)S(1)}, u32[]{:S(2)}, u32[]{:S(2)}) collective-permute-start(bf16[24,4096]{1,0:T(8,128)(2,1)S(1)} %get-tuple-element.487), channel_id=1, source_target_pairs={{0,32},{32,64},{64,96},{96,128},{128,160},{160,192},{192,224},{224... | collective-permute-start | bytes 589832 | tf_op jit(solution)/shard_map/while/body/eval_jaxpr/ppermute | solution.py:9
  700.1 10.4 %collective-permute-start = (bf16[24,4096]{1,0:T(8,128)(2,1)S(1)}, bf16[24,4096]{1,0:T(8,128)(2,1)S(1)}, u32[]{:S(2)}, u32[]{:S(2)}) collective-permute-start(bf16[24,4096]{1,0:T(8,128)(2,1)S(1)} %get-tuple-element.487), channel_id=1, source_target_pairs={{0,32},{32,64},{64,96},{96,128},{128,160},{160,192},{192,224},{224... | collective-permute-start | bytes 589832 | tf_op jit(solution)/shard_map/while/body/eval_jaxpr/ppermute | solution.py:9
  711.5 9.5 %collective-permute-start = (bf16[24,4096]{1,0:T(8,128)(2,1)S(1)}, bf16[24,4096]{1,0:T(8,128)(2,1)S(1)}, u32[]{:S(2)}, u32[]{:S(2)}) collective-permute-start(bf16[24,4096]{1,0:T(8,128)(2,1)S(1)} %get-tuple-element.487), channel_id=1, source_target_pairs={{0,32},{32,64},{64,96},{96,128},{128,160},{160,192},{192,224},{224... | collective-permute-start | bytes 589832 | tf_op jit(solution)/shard_map/while/body/eval_jaxpr/ppermute | solution.py:9
  722.1 9.4 %collective-permute-start = (bf16[24,4096]{1,0:T(8,128)(2,1)S(1)}, bf16[24,4096]{1,0:T(8,128)(2,1)S(1)}, u32[]{:S(2)}, u32[]{:S(2)}) collective-permute-start(bf16[24,4096]{1,0:T(8,128)(2,1)S(1)} %get-tuple-element.487), channel_id=1, source_target_pairs={{0,32},{32,64},{64,96},{96,128},{128,160},{160,192},{192,224},{224... | collective-permute-start | bytes 589832 | tf_op jit(solution)/shard_map/while/body/eval_jaxpr/ppermute | solution.py:9
  732.6 9.3 %collective-permute-start = (bf16[24,4096]{1,0:T(8,128)(2,1)S(1)}, bf16[24,4096]{1,0:T(8,128)(2,1)S(1)}, u32[]{:S(2)}, u32[]{:S(2)}) collective-permute-start(bf16[24,4096]{1,0:T(8,128)(2,1)S(1)} %get-tuple-element.487), channel_id=1, source_target_pairs={{0,32},{32,64},{64,96},{96,128},{128,160},{160,192},{192,224},{224... | collective-permute-start | bytes 589832 | tf_op jit(solution)/shard_map/while/body/eval_jaxpr/ppermute | solution.py:9
  743.0 0.7 copy-start
Sparse Core Ops, SparseCore 0:
  9.2 75.0 all-gather.3
  86.2 72.1 all-gather.5
  160.2 88.7 all-gather.7
where the time goes:
time: 765 us; the launch traced here: 750 us
  waiting for transfers between devices  265 us (35%)
  starting transfers between devices  199 us (26%)
  matrix products  124 us (16%)
  loops' own time  61.7 us (8%)
  local copies, waits for them, and re-layouts  52.5 us (7%)
  other arithmetic  34.6 us (5%)
  between operations  13.1 us (2%)
    ppermute x31, starting transfers between devices, shifted(): lax.ppermute(value, axis, [(i, (i + by) % count) for i in range(count)])  199 us
    all_gather x1, waiting for transfers between devices, local(): lax.all_gather(proj_out, 'fsdp', axis=2, tiled=True)  90.6 us
    dot_general x16, matrix products, advance(): jnp.dot(hidden, w_second, preferred_element_type=jnp.float32)  77.2 us
    all_gather x1, waiting for transfers between devices, local(): lax.all_gather(proj_gate, 'fsdp', axis=1, tiled=True)  75.6 us
    all_gather x1, waiting for transfers between devices, local(): lax.all_gather(proj_in, 'fsdp', axis=1, tiled=True)  74.1 us
    another operation x1, loops' own time, local(): lax.fori_loop(0, total_steps, make_step(full_gate, full_first, full_secon...  61 us
    dot_general x16, matrix products, advance(): jnp.dot(normed, w_gate, preferred_element_type=jnp.float32)  46.5 us
    dynamic_slice x31, local copies, waits for them, and re-layouts, entering(): picked = lax.dynamic_index_in_dim(plan, slot, 0, keepdims=False)  39.1 us
  transfers between devices with their start and end apart: 34, of which 14 were waited for; matrix products, arithmetic and copies ran while one was open for 5% of the time, Pallas kernels for 0%

commit v1 on v0

v1 whole, which is shorter than its diff:
```python
import functools

import jax
import jax.numpy as jnp
from jax import lax
from jax.experimental import pallas as pl
from jax.experimental.pallas import tpu as pltpu
from jax.sharding import PartitionSpec as P

MESH = pl.DeviceIdType.MESH
PIPE, FSDP, ZN = 8, 32, 8
D, H, SLICE = 4096, 512, 128
LAPS, MB, TOK = 2, 8, 24
GROUP = 16
GROUPS = MB * TOK // GROUP
CHUNKS = 4
CW = D // CHUNKS
STEPS, LINKS, KINDS = 5, 3, 3
EPS = 1e-05


def kernel(
    plan_ref,
    inputs_ref,
    gains_ref,
    gate_ref,
    first_ref,
    second_ref,
    o_ref,
    w_gate,
    w_first,
    w_second,
    staged,
    xbuf,
    landing,
    stage_sem,
    own_sem,
    gather_send,
    gather_recv,
    pair_send,
    pair_recv,
    x_send,
    x_recv,
    end_send,
    end_recv,
):
    p = lax.axis_index("pipe")
    f = lax.axis_index("fsdp")
    y = f // 16
    z = (f // 2) % ZN
    core = f % 2

    def shard(other, dz):
        row = 1 - y if other else y
        return row * 16 + ((z + dz + ZN) % ZN) * 2 + core

    up, down, across = (p, shard(0, 1)), (p, shard(0, -1)), (p, shard(1, 0))
    twin = (p, f + 1 - 2 * core)
    targets = (up, down, across)

    barrier = pltpu.get_barrier_semaphore()
    for device in (up, down, across, twin):
        pl.semaphore_signal(barrier, inc=1, device_id=device, device_id_type=MESH)
    for ahead in range(1, PIPE):
        pl.semaphore_signal(
            barrier, inc=1, device_id=((p + ahead) % PIPE, f), device_id_type=MESH
        )
    pl.semaphore_wait(barrier, 4 + PIPE - 1)

    sends = (
        ((0, 0), (0, -1), (0, -2), (0, -3), (1, -3)),
        ((0, 0), (0, 1), (0, 2), (1, 0), (1, 1)),
        ((0, 0), (0, -1), (0, -2), (0, -3), (0, 3)),
    )
    gets = (
        ((0, -1), (0, -2), (0, -3), (0, -4), (1, -4)),
        ((0, 1), (0, 2), (0, 3), (1, 1), (1, 2)),
        ((1, 0), (1, -1), (1, -2), (1, -3), (1, 3)),
    )

    def place(kind, lap, index):
        part = pl.ds(pl.multiple_of(index * SLICE, SLICE), SLICE)
        if kind == 0:
            return w_gate.at[lap, part, :]
        if kind == 1:
            return w_first.at[lap, part, :]
        return w_second.at[lap, :, part]

    def own(kind, lap):
        return (gate_ref, first_ref, second_ref)[kind].at[lap]

    def bulk(kind, lap, shards):
        if kind == 0:
            return w_gate.at[lap, pl.ds(0, shards * SLICE), :]
        if kind == 1:
            return w_first.at[lap, pl.ds(0, shards * SLICE), :]
        return w_second.at[lap, :, pl.ds(0, shards * SLICE)]

    def send(lap, step, kind):
        for link in range(LINKS):
            index = shard(*sends[link][step])
            source = own(kind, lap) if step == 0 else place(kind, lap, index)
            pltpu.make_async_remote_copy(
                src_ref=source,
                dst_ref=place(kind, lap, index),
                send_sem=gather_send.at[lap, link, kind],
                recv_sem=gather_recv.at[lap, link, step, kind],
                device_id=targets[link],
                device_id_type=MESH,
            ).start()

    def to_twin(lap, kind, index, source):
        pltpu.make_async_remote_copy(
            src_ref=source,
            dst_ref=place(kind, lap, index),
            send_sem=pair_send.at[lap, kind],
            recv_sem=pair_recv.at[lap, kind],
            device_id=twin,
            device_id_type=MESH,
        ).start()

    def keep_own(lap, kind):
        return pltpu.make_async_copy(own(kind, lap), place(kind, lap, f), own_sem.at[lap, kind])

    def gather_begin(lap):
        for kind in range(KINDS):
            send(lap, 0, kind)
        for kind in range(KINDS):
            to_twin(lap, kind, f, own(kind, lap))
            keep_own(lap, kind).start()

    def gather_step(lap, step, kind):
        for link in range(LINKS):
            target = place(kind, lap, shard(*gets[link][step]))
            pltpu.make_async_remote_copy(
                src_ref=target,
                dst_ref=target,
                send_sem=gather_send.at[lap, link, kind],
                recv_sem=gather_recv.at[lap, link, step, kind],
                device_id=targets[link],
                device_id_type=MESH,
            ).wait_recv()
        if step + 1 < STEPS:
            send(lap, step + 1, kind)
        for link in range(LINKS):
            index = shard(*gets[link][step])
            to_twin(lap, kind, index, place(kind, lap, index))

    def gather_end(lap):
        for kind in range(KINDS):
            whole = bulk(kind, lap, 16)
            pltpu.make_async_remote_copy(
                src_ref=whole,
                dst_ref=whole,
                send_sem=pair_send.at[lap, kind],
                recv_sem=pair_recv.at[lap, kind],
                device_id=twin,
                device_id_type=MESH,
            ).wait_recv()
            keep_own(lap, kind).wait()

    def gather_drain(lap):
        for kind in range(KINDS):
            for link in range(LINKS):
                part = bulk(kind, lap, STEPS)
                pltpu.make_async_remote_copy(
                    src_ref=part,
                    dst_ref=part,
                    send_sem=gather_send.at[lap, link, kind],
                    recv_sem=gather_recv.at[lap, link, 0, kind],
                    device_id=targets[link],
                    device_id_type=MESH,
                ).wait_send()
            whole = bulk(kind, lap, 16)
            pltpu.make_async_remote_copy(
                src_ref=whole,
                dst_ref=whole,
                send_sem=pair_send.at[lap, kind],
                recv_sem=pair_recv.at[lap, kind],
                device_id=twin,
                device_id_type=MESH,
            ).wait_send()

    order = [(step, kind) for step in range(STEPS) for kind in range(KINDS)]

    gather_begin(0)

    @pl.when(p == 0)
    def _():
        stage = pltpu.make_async_copy(inputs_ref, staged, stage_sem)
        stage.start()
        stage.wait()
        for pair in range(MB // 2):
            even = staged[plan_ref[2 * pair]].astype(jnp.float32)
            odd = staged[plan_ref[2 * pair + 1]].astype(jnp.float32)
            xbuf[0, 3 * pair] = even[:16].astype(jnp.bfloat16)
            xbuf[0, 3 * pair + 1] = jnp.concatenate([even[16:], odd[:8]], axis=0).astype(
                jnp.bfloat16
            )
            xbuf[0, 3 * pair + 2] = odd[8:].astype(jnp.bfloat16)

    for step, kind in order:
        gather_step(0, step, kind)
    gather_begin(1)
    gather_end(0)

    onward = ((p + 1) % PIPE, f)

    def columns(chunk):
        return pl.ds(chunk * CW, CW)

    def hop(lap, group, chunk, to_lap):
        return pltpu.make_async_remote_copy(
            src_ref=xbuf.at[lap, group, :, columns(chunk)],
            dst_ref=xbuf.at[to_lap, group, :, columns(chunk)],
            send_sem=x_send.at[lap, group],
            recv_sem=x_recv.at[to_lap, group, chunk],
            device_id=onward,
            device_id_type=MESH,
        )

    def finish(group, second, slot):
        return pltpu.make_async_remote_copy(
            src_ref=xbuf.at[1, group],
            dst_ref=landing.at[1 - second if second else jnp.where(group % 3 == 0, 0, 1)],
            send_sem=end_send.at[second, group],
            recv_sem=end_recv.at[1 - second if second else jnp.where(group % 3 == 0, 0, 1)],
            device_id=(slot, f),
            device_id_type=MESH,
        )

    def slots(group):
        pair = group // 3
        return 2 * pair + jnp.where(group % 3 == 2, 1, 0), 2 * pair + 1

    def one(turn, carry):
        lap = turn // GROUPS
        group = turn % GROUPS
        for number in range(GROUPS):
            @pl.when(turn == number)
            def _():
                gather_step(1, *order[number])

        @pl.when(turn == GROUPS)
        def _():
            for step, kind in order[GROUPS:]:
                gather_step(1, step, kind)
            gather_end(1)

        total_gate = jnp.zeros((GROUP, H), jnp.float32)
        total_first = jnp.zeros((GROUP, H), jnp.float32)
        squares = jnp.zeros((GROUP, 1), jnp.float32)
        for chunk in range(CHUNKS):
            @pl.when((p > 0) | (lap > 0))
            def _():
                hop(lap, group, chunk, lap).wait_recv()

            wide = xbuf[lap, group, :, columns(chunk)].astype(jnp.float32)
            squares += jnp.sum(wide * wide, axis=-1, keepdims=True)
            scaled = (wide * gains_ref[pl.ds(lap, 1), columns(chunk)]).astype(jnp.bfloat16)
            total_gate += jnp.dot(
                scaled, w_gate[lap, columns(chunk), :], preferred_element_type=jnp.float32
            )
            total_first += jnp.dot(
                scaled, w_first[lap, columns(chunk), :], preferred_element_type=jnp.float32
            )
        scale = lax.rsqrt(squares * (1.0 / D) + EPS)
        gate = total_gate * scale
        hidden = (gate / (1.0 + jnp.exp(-gate)) * (total_first * scale)).astype(jnp.bfloat16)
        last = (p == PIPE - 1) & (lap == 1)
        to_lap = jnp.where(p == PIPE - 1, 1, lap)
        for chunk in range(CHUNKS):
            wide = xbuf[lap, group, :, columns(chunk)].astype(jnp.float32)
            wide += jnp.dot(
                hidden, w_second[lap, :, columns(chunk)], preferred_element_type=jnp.float32
            )
            xbuf[lap, group, :, columns(chunk)] = wide.astype(jnp.bfloat16)

            @pl.when(jnp.logical_not(last))
            def _():
                hop(lap, group, chunk, to_lap).start()

        slot, after = slots(group)

        @pl.when(last & (group < GROUPS - 1))
        def _():
            finish(group, 0, slot).start()

        @pl.when(last & (group % 3 == 1) & (group < GROUPS - 2))
        def _():
            finish(group, 1, after).start()

        return carry

    lax.fori_loop(0, LAPS * GROUPS, one, 0)

    def put(head, tail):
        head, tail = head.astype(jnp.float32), tail.astype(jnp.float32)

        @pl.when(p % 2 == 0)
        def _():
            o_ref[0] = jnp.concatenate([head, tail[:8]], axis=0).astype(jnp.bfloat16)

        @pl.when(p % 2 == 1)
        def _():
            o_ref[0] = jnp.concatenate([head[8:], tail], axis=0).astype(jnp.bfloat16)

    @pl.when(p < PIPE - 1)
    def _():
        for place_in in range(2):
            pltpu.make_async_remote_copy(
                src_ref=landing.at[place_in],
                dst_ref=landing.at[place_in],
                send_sem=end_send.at[0, 0],
                recv_sem=end_recv.at[place_in],
                device_id=onward,
                device_id_type=MESH,
            ).wait_recv()
        put(landing[0], landing[1])

    @pl.when(p == PIPE - 1)
    def _():
        put(xbuf[1, GROUPS - 2], xbuf[1, GROUPS - 1])

    for lap in range(LAPS):
        gather_drain(lap)

    def sent(turn, carry):
        lap = turn // GROUPS
        group = turn % GROUPS
        last = (p == PIPE - 1) & (lap == 1)

        @pl.when(jnp.logical_not(last))
        def _():
            pltpu.make_async_remote_copy(
                src_ref=xbuf.at[lap, group],
                dst_ref=xbuf.at[lap, group],
                send_sem=x_send.at[lap, group],
                recv_sem=x_recv.at[lap, group, 0],
                device_id=onward,
                device_id_type=MESH,
            ).wait_send()

        @pl.when(last & (group < GROUPS - 1))
        def _():
            finish(group, 0, 0).wait_send()

        @pl.when(last & (group % 3 == 1) & (group < GROUPS - 2))
        def _():
            finish(group, 1, 0).wait_send()

        return carry

    lax.fori_loop(0, LAPS * GROUPS, sent, 0)


def local(inputs, gains, proj_gate, proj_in, proj_out, plan):
    anywhere = pl.BlockSpec(memory_space=pl.ANY)
    vmem = pl.BlockSpec(memory_space=pltpu.VMEM)
    dma = pltpu.SemaphoreType.DMA
    rows = MB * TOK
    return pl.pallas_call(
        kernel,
        out_shape=jax.ShapeDtypeStruct((1, TOK, D), jnp.bfloat16),
        in_specs=[
            pl.BlockSpec(memory_space=pltpu.SMEM),
            anywhere,
            vmem,
            anywhere,
            anywhere,
            anywhere,
        ],
        out_specs=vmem,
        scratch_shapes=[
            pltpu.VMEM((LAPS, D, H), jnp.bfloat16),
            pltpu.VMEM((LAPS, D, H), jnp.bfloat16),
            pltpu.VMEM((LAPS, H, D), jnp.bfloat16),
            pltpu.VMEM((MB, TOK, D), jnp.bfloat16),
            pltpu.VMEM((LAPS, GROUPS, GROUP, D), jnp.bfloat16),
            pltpu.VMEM((2, GROUP, D), jnp.bfloat16),
            dma,
            dma((LAPS, KINDS)),
            dma((LAPS, LINKS, KINDS)),
            dma((LAPS, LINKS, STEPS, KINDS)),
            dma((LAPS, KINDS)),
            dma((LAPS, KINDS)),
            dma((LAPS, GROUPS)),
            dma((LAPS, GROUPS, CHUNKS)),
            dma((2, GROUPS)),
            dma((2,)),
        ],
        compiler_params=pltpu.CompilerParams(
            collective_id=0, has_side_effects=True, vmem_limit_bytes=56 << 20
        ),
        cost_estimate=pl.CostEstimate(
            flops=LAPS * rows * D * H * 6, bytes_accessed=LAPS * D * H * 6, transcendentals=0
        ),
        name="sections",
    )(plan, inputs, gains, proj_gate, proj_in, proj_out)


def solution(mesh):
    in_specs = (
        P(None, "fsdp", None),
        P("pipe", None),
        P("pipe", "fsdp", None),
        P("pipe", "fsdp", None),
        P("pipe", None, "fsdp"),
        P(),
    )
    out_specs = P("pipe", "fsdp", None)
    return jax.shard_map(local, mesh=mesh, in_specs=in_specs, out_specs=out_specs, check_vma=False)
```

time: 765 us -> 205 us (0.27); the launches traced: 750 us -> 203 us
  waiting for transfers between devices: 265 us -> 0 us
  Pallas kernels: 0 us -> 201 us
  starting transfers between devices: 199 us -> 0 us
  matrix products: 124 us -> 0 us
  loops' own time: 61.7 us -> 0 us
  local copies, waits for them, and re-layouts: 52.5 us -> 1.62 us
  other arithmetic: 34.6 us -> 0 us
  between operations: 13.1 us -> 0.01 us
    all_gather x3 -> x0, waiting for transfers between devices: 240 us -> none  [the longest x1 90.6 us: local(): lax.all_gather(proj_out, 'fsdp', axis=2, tiled=True)]
    pallas_call x0 -> x1, Pallas kernels: none -> 201 us  [local(): pl.pallas_call(kernel, out_shape=jax.ShapeDtypeStruct((1, TOK, D), jnp.bf...]
    ppermute x31 -> x0, starting transfers between devices: 199 us -> none  [shifted(): lax.ppermute(value, axis, [(i, (i + by) % count) for i in range(count)])]
    dot_general x32 -> x0, matrix products: 124 us -> none  [the longest x16 77.2 us: advance(): jnp.dot(hidden, w_second, preferred_element_type=jnp.float32)]
    another operation x32 -> x0, loops' own time: 61.7 us -> none  [the longest x1 61 us: local(): lax.fori_loop(0, total_steps, make_step(full_gate, full_first, full_secon...]
    dynamic_slice x47 -> x0, local copies, waits for them, and re-layouts: 51.5 us -> none  [the longest x31 39.1 us: entering(): picked = lax.dynamic_index_in_dim(plan, slot, 0, keepdims=False)]
    select_n x31 -> x0, other arithmetic: 31.9 us -> none  [one_step(): return (moved, jnp.where(keep, source, result))]
    ppermute x31 -> x0, waiting for transfers between devices: 23 us -> none  [shifted(): lax.ppermute(value, axis, [(i, (i + by) % count) for i in range(count)])]
  transfers between devices with their start and end apart: 34 -> 0, of which waited for: 14 -> 0; matrix products, arithmetic and copies ran while one was open for 5% -> 0% of each run, Pallas kernels for 0% -> 0%
where the time goes in v1:
time: 205 us; the launch traced here: 203 us
  Pallas kernels  201 us (98%)
    pallas_call x1, Pallas kernels, local(): pl.pallas_call(kernel, out_shape=jax.ShapeDtypeStruct((1, TOK, D), jnp.bf...  201 us

profile of v1, /device:TPU:20, one launch (start us, length us, event | category | flops | bytes accessed | tf_op | source)
XLA Modules:
  0.0 202.7 jit_solution(10978194537072415979)
XLA Ops:
  0.0 201.1 %sections.1 = bf16[1,24,4096]{2,1,0:T(8,128)(2,1)} custom-call(s32[8]{0:T(128)} %plan_ref.1, bf16[8,24,4096]{2,1,0:T(8,128)(2,1)} %inputs_ref.1, f32[2,4096]{1,0:T(2,128)} %gains_ref.1, bf16[2,128,512]{2,1,0:T(8,128)(2,1)} %gate_ref.1, bf16[2,128,512]{2,1,0:T(8,128)(2,1)} %first_ref.1, bf16[2,512,128]{2,1,0:T(8,128)(2,1)} %second_ref.1), custom_call_target="tpu_custom_call" | custom-call | flops 4831838208 | bytes 25165824 | tf_op jit(solution)/shard_map/sections/pallas_call | solution.py:362
  201.1 1.6 copy.8

commit v2 on v1

--- a/solution.py
+++ b/solution.py
@@ -16,6 +16,8 @@
 CHUNKS = 4
 CW = D // CHUNKS
 STEPS, LINKS, KINDS = 5, 3, 3
+ROUNDS = STEPS * KINDS
+EARLY = 2
 EPS = 1e-05
 
 
@@ -51,7 +53,7 @@
     core = f % 2
 
     def shard(other, dz):
-        row = 1 - y if other else y
+        row = (y + other) % 2
         return row * 16 + ((z + dz + ZN) % ZN) * 2 + core
 
     up, down, across = (p, shard(0, 1)), (p, shard(0, -1)), (p, shard(1, 0))
@@ -65,18 +67,36 @@
         pl.semaphore_signal(
             barrier, inc=1, device_id=((p + ahead) % PIPE, f), device_id_type=MESH
         )
-    pl.semaphore_wait(barrier, 4 + PIPE - 1)
-
-    sends = (
+    for ahead in (1, PIPE - 1):
+        pl.semaphore_signal(
+            barrier,
+            inc=1,
+            device_id=((p + ahead) % PIPE, shard(1, 0)),
+            device_id_type=MESH,
+        )
+    pl.semaphore_wait(barrier, 4 + PIPE - 1 + 2)
+
+    plan = (
         ((0, 0), (0, -1), (0, -2), (0, -3), (1, -3)),
         ((0, 0), (0, 1), (0, 2), (1, 0), (1, 1)),
         ((0, 0), (0, -1), (0, -2), (0, -3), (0, 3)),
     )
-    gets = (
-        ((0, -1), (0, -2), (0, -3), (0, -4), (1, -4)),
-        ((0, 1), (0, 2), (0, 3), (1, 1), (1, 2)),
-        ((1, 0), (1, -1), (1, -2), (1, -3), (1, 3)),
-    )
+    moves = ((0, -1), (0, 1), (1, 0))
+
+    def pick(link, step, part):
+        if isinstance(step, int):
+            return plan[link][step][part]
+        found = plan[link][0][part]
+        for number in range(1, STEPS):
+            found = jnp.where(step == number, plan[link][number][part], found)
+        return found
+
+    def sent_shard(link, step):
+        return shard(pick(link, step, 0), pick(link, step, 1))
+
+    def got_shard(link, step):
+        other, dz = moves[link]
+        return shard(pick(link, step, 0) + other, pick(link, step, 1) + dz)
 
     def place(kind, lap, index):
         part = pl.ds(pl.multiple_of(index * SLICE, SLICE), SLICE)
@@ -97,11 +117,11 @@
         return w_second.at[lap, :, pl.ds(0, shards * SLICE)]
 
     def send(lap, step, kind):
+        fresh = isinstance(step, int) and step == 0
         for link in range(LINKS):
-            index = shard(*sends[link][step])
-            source = own(kind, lap) if step == 0 else place(kind, lap, index)
+            index = f if fresh else sent_shard(link, step)
             pltpu.make_async_remote_copy(
-                src_ref=source,
+                src_ref=own(kind, lap) if fresh else place(kind, lap, index),
                 dst_ref=place(kind, lap, index),
                 send_sem=gather_send.at[lap, link, kind],
                 recv_sem=gather_recv.at[lap, link, step, kind],
@@ -131,7 +151,7 @@
 
     def gather_step(lap, step, kind):
         for link in range(LINKS):
-            target = place(kind, lap, shard(*gets[link][step]))
+            target = place(kind, lap, got_shard(link, step))
             pltpu.make_async_remote_copy(
                 src_ref=target,
                 dst_ref=target,
@@ -140,24 +160,26 @@
                 device_id=targets[link],
                 device_id_type=MESH,
             ).wait_recv()
-        if step + 1 < STEPS:
-            send(lap, step + 1, kind)
+        if isinstance(step, int):
+            if step + 1 < STEPS:
+                send(lap, step + 1, kind)
+        else:
+            pl.when(step + 1 < STEPS)(functools.partial(send, lap, step + 1, kind))
         for link in range(LINKS):
-            index = shard(*gets[link][step])
+            index = got_shard(link, step)
             to_twin(lap, kind, index, place(kind, lap, index))
 
-    def gather_end(lap):
-        for kind in range(KINDS):
-            whole = bulk(kind, lap, 16)
-            pltpu.make_async_remote_copy(
-                src_ref=whole,
-                dst_ref=whole,
-                send_sem=pair_send.at[lap, kind],
-                recv_sem=pair_recv.at[lap, kind],
-                device_id=twin,
-                device_id_type=MESH,
-            ).wait_recv()
-            keep_own(lap, kind).wait()
+    def gather_end(lap, kind):
+        whole = bulk(kind, lap, 16)
+        pltpu.make_async_remote_copy(
+            src_ref=whole,
+            dst_ref=whole,
+            send_sem=pair_send.at[lap, kind],
+            recv_sem=pair_recv.at[lap, kind],
+            device_id=twin,
+            device_id_type=MESH,
+        ).wait_recv()
+        keep_own(lap, kind).wait()
 
     def gather_drain(lap):
         for kind in range(KINDS):
@@ -181,8 +203,6 @@
                 device_id_type=MESH,
             ).wait_send()
 
-    order = [(step, kind) for step in range(STEPS) for kind in range(KINDS)]
-
     gather_begin(0)
 
     @pl.when(p == 0)
@@ -199,23 +219,39 @@
             )
             xbuf[0, 3 * pair + 2] = odd[8:].astype(jnp.bfloat16)
 
-    for step, kind in order:
-        gather_step(0, step, kind)
-    gather_begin(1)
-    gather_end(0)
+    for step in range(STEPS):
+        for kind in range(KINDS):
+            gather_step(0, step, kind)
+        if step == STEPS - 2:
+            gather_begin(1)
+    for kind in range(KINDS - 1):
+        gather_end(0, kind)
+
+    def next_lap(number, carry):
+        for kind in range(KINDS):
+            @pl.when(number % KINDS == kind)
+            def _():
+                gather_step(1, number // KINDS, kind)
+
+        return carry
+
+    early = EARLY * p
+    lax.fori_loop(0, early, next_lap, 0)
 
     onward = ((p + 1) % PIPE, f)
+    turned = ((p + 1) % PIPE, shard(1, 0))
+    crossing = (p % 4) == 3
 
     def columns(chunk):
         return pl.ds(chunk * CW, CW)
 
-    def hop(lap, group, chunk, to_lap):
+    def hop(lap, group, chunk, to_lap, device):
         return pltpu.make_async_remote_copy(
             src_ref=xbuf.at[lap, group, :, columns(chunk)],
             dst_ref=xbuf.at[to_lap, group, :, columns(chunk)],
             send_sem=x_send.at[lap, group],
             recv_sem=x_recv.at[to_lap, group, chunk],
-            device_id=onward,
+            device_id=device,
             device_id_type=MESH,
         )
 
@@ -236,16 +272,17 @@
     def one(turn, carry):
         lap = turn // GROUPS
         group = turn % GROUPS
-        for number in range(GROUPS):
-            @pl.when(turn == number)
-            def _():
-                gather_step(1, *order[number])
+        step = early + turn - 1
+
+        @pl.when((turn > 0) & (turn < GROUPS) & (step < ROUNDS))
+        def _():
+            next_lap(step, 0)
 
         @pl.when(turn == GROUPS)
         def _():
-            for step, kind in order[GROUPS:]:
-                gather_step(1, step, kind)
-            gather_end(1)
+            lax.fori_loop(jnp.minimum(step, ROUNDS), ROUNDS, next_lap, 0)
+            for kind in range(KINDS):
+                gather_end(1, kind)
 
         total_gate = jnp.zeros((GROUP, H), jnp.float32)
         total_first = jnp.zeros((GROUP, H), jnp.float32)
@@ -253,7 +290,7 @@
         for chunk in range(CHUNKS):
             @pl.when((p > 0) | (lap > 0))
             def _():
-                hop(lap, group, chunk, lap).wait_recv()
+                hop(lap, group, chunk, lap, onward).wait_recv()
 
             wide = xbuf[lap, group, :, columns(chunk)].astype(jnp.float32)
             squares += jnp.sum(wide * wide, axis=-1, keepdims=True)
@@ -267,8 +304,14 @@
         scale = lax.rsqrt(squares * (1.0 / D) + EPS)
         gate = total_gate * scale
         hidden = (gate / (1.0 + jnp.exp(-gate)) * (total_first * scale)).astype(jnp.bfloat16)
+
+        @pl.when(turn == 0)
+        def _():
+            gather_end(0, KINDS - 1)
+
         last = (p == PIPE - 1) & (lap == 1)
         to_lap = jnp.where(p == PIPE - 1, 1, lap)
+        turning = crossing & (lap == 0)
         for chunk in range(CHUNKS):
             wide = xbuf[lap, group, :, columns(chunk)].astype(jnp.float32)
             wide += jnp.dot(
@@ -276,9 +319,13 @@
             )
             xbuf[lap, group, :, columns(chunk)] = wide.astype(jnp.bfloat16)
 
-            @pl.when(jnp.logical_not(last))
+            @pl.when(jnp.logical_not(last | turning))
             def _():
-                hop(lap, group, chunk, to_lap).start()
+                hop(lap, group, chunk, to_lap, onward).start()
+
+            @pl.when(turning)
+            def _():
+                hop(lap, group, chunk, to_lap, turned).start()
 
         slot, after = slots(group)
 

time: 205 us -> 180 us (0.88); the launches traced: 203 us -> 180 us
  Pallas kernels: 201 us -> 179 us
    pallas_call x1, Pallas kernels: 201 us -> 179 us  [local(): pl.pallas_call(kernel, out_shape=jax.ShapeDtypeStruct((1, TOK, D), jnp.bf...]
where the time goes in v2:
time: 180 us
  Pallas kernels  179 us (99%)
    pallas_call x1, Pallas kernels, local(): pl.pallas_call(kernel, out_shape=jax.ShapeDtypeStruct((1, TOK, D), jnp.bf...  179 us

profile of v2, /device:TPU:20, one launch (start us, length us, event | category | flops | bytes accessed | tf_op | source)
XLA Modules:
  0.0 180.2 jit_solution(3450145018927759415)
XLA Ops:
  0.0 178.6 %sections.1 = bf16[1,24,4096]{2,1,0:T(8,128)(2,1)} custom-call(s32[8]{0:T(128)} %plan_ref.1, bf16[8,24,4096]{2,1,0:T(8,128)(2,1)} %inputs_ref.1, f32[2,4096]{1,0:T(2,128)} %gains_ref.1, bf16[2,128,512]{2,1,0:T(8,128)(2,1)} %gate_ref.1, bf16[2,128,512]{2,1,0:T(8,128)(2,1)} %first_ref.1, bf16[2,512,128]{2,1,0:T(8,128)(2,1)} %second_ref.1), custom_call_target="tpu_custom_call" | custom-call | flops 4831838208 | bytes 25165824 | tf_op jit(solution)/shard_map/sections/pallas_call | solution.py:409
  178.6 1.6 copy.8

commit v3 on v2

--- a/solution.py
+++ b/solution.py
@@ -13,11 +13,15 @@
 LAPS, MB, TOK = 2, 8, 24
 GROUP = 16
 GROUPS = MB * TOK // GROUP
-CHUNKS = 4
+MOVED = 2
+MOST = GROUPS + MOVED
+CHUNKS = 8
 CW = D // CHUNKS
 STEPS, LINKS, KINDS = 5, 3, 3
 ROUNDS = STEPS * KINDS
 EARLY = 2
+LATER = 6
+RELAYED = 2
 EPS = 1e-05
 
 
@@ -33,8 +37,11 @@
     w_first,
     w_second,
     staged,
+    ordered,
     xbuf,
     landing,
+    passing,
+    passing_second,
     stage_sem,
     own_sem,
     gather_send,
@@ -45,6 +52,9 @@
     x_recv,
     end_send,
     end_recv,
+    over_send,
+    relay_send,
+    relay_recv,
 ):
     p = lax.axis_index("pipe")
     f = lax.axis_index("fsdp")
@@ -61,29 +71,64 @@
     targets = (up, down, across)
 
     barrier = pltpu.get_barrier_semaphore()
+    def greet(device):
+        pl.semaphore_signal(barrier, inc=1, device_id=device, device_id_type=MESH)
+
+    other = twin[1]
+    before, after = (p + PIPE - 1) % PIPE, (p + 1) % PIPE
     for device in (up, down, across, twin):
-        pl.semaphore_signal(barrier, inc=1, device_id=device, device_id_type=MESH)
-    for ahead in range(1, PIPE):
-        pl.semaphore_signal(
-            barrier, inc=1, device_id=((p + ahead) % PIPE, f), device_id_type=MESH
-        )
-    for ahead in (1, PIPE - 1):
-        pl.semaphore_signal(
-            barrier,
-            inc=1,
-            device_id=((p + ahead) % PIPE, shard(1, 0)),
-            device_id_type=MESH,
-        )
-    pl.semaphore_wait(barrier, 4 + PIPE - 1 + 2)
-
-    plan = (
+        greet(device)
+    mate = ((p + PIPE // 2) % PIPE, shard(1, 0))
+    greet(mate)
+    for section in (before, after):
+        greet((section, f))
+        greet((section, shard(1, 0)))
+
+    @pl.when(p == PIPE - 1)
+    def _():
+        for section in range(PIPE - 1):
+            greet((section, other))
+            if 0 < section < PIPE - 2:
+                greet((section, f))
+
+    @pl.when(p < PIPE - 1)
+    def _():
+        greet((PIPE - 1, other))
+
+    @pl.when((p > 0) & (p < PIPE - 2))
+    def _():
+        greet((PIPE - 1, f))
+
+    @pl.when(p == PIPE - 1)
+    def _():
+        pl.semaphore_wait(barrier, 9 + 2 * PIPE - 4)
+
+    @pl.when((p > 0) & (p < PIPE - 2))
+    def _():
+        pl.semaphore_wait(barrier, 9 + 2)
+
+    @pl.when((p == 0) | (p == PIPE - 2))
+    def _():
+        pl.semaphore_wait(barrier, 9 + 1)
+
+    even = (
         ((0, 0), (0, -1), (0, -2), (0, -3), (1, -3)),
         ((0, 0), (0, 1), (0, 2), (1, 0), (1, 1)),
         ((0, 0), (0, -1), (0, -2), (0, -3), (0, 3)),
     )
+    hurried = (
+        ((0, 0), (0, -1), (0, -2), (0, -3), (1, -3)),
+        ((0, 0), (0, 1), (0, 2), (1, 2), (1, 3)),
+        ((0, 0), (0, 1), (0, 2), (0, -3), (0, -4)),
+    )
+    patient = (
+        ((0, 0), (0, -1), (0, -2), (0, -3), (1, 0), (1, -1)),
+        ((0, 0), (0, 1), (0, 2), (1, 0), (1, 1), (1, 2)),
+        ((0, 0), None, None, None, (0, -3), (0, -4)),
+    )
     moves = ((0, -1), (0, 1), (1, 0))
 
-    def pick(link, step, part):
+    def pick(plan, link, step, part):
         if isinstance(step, int):
             return plan[link][step][part]
         found = plan[link][0][part]
@@ -91,12 +136,23 @@
             found = jnp.where(step == number, plan[link][number][part], found)
         return found
 
-    def sent_shard(link, step):
-        return shard(pick(link, step, 0), pick(link, step, 1))
-
-    def got_shard(link, step):
+    def sent_shard(plan, link, step):
+        return shard(pick(plan, link, step, 0), pick(plan, link, step, 1))
+
+    def got_shard(plan, link, step):
         other, dz = moves[link]
-        return shard(pick(link, step, 0) + other, pick(link, step, 1) + dz)
+        return shard(pick(plan, link, step, 0) + other, pick(plan, link, step, 1) + dz)
+
+    def used(plan, step, kind):
+        if not isinstance(step, int):
+            return range(LINKS)
+        links = [link for link in range(LINKS) if step < len(plan[link]) and plan[link][step]]
+        if plan is hurried and step == STEPS - 1:
+            links = [kind]
+        return links
+
+    def count(plan, link, kind):
+        return sum(link in used(plan, step, kind) for step in range(len(plan[link])))
 
     def place(kind, lap, index):
         part = pl.ds(pl.multiple_of(index * SLICE, SLICE), SLICE)
@@ -116,10 +172,10 @@
             return w_first.at[lap, pl.ds(0, shards * SLICE), :]
         return w_second.at[lap, :, pl.ds(0, shards * SLICE)]
 
-    def send(lap, step, kind):
+    def send(plan, lap, step, kind):
         fresh = isinstance(step, int) and step == 0
-        for link in range(LINKS):
-            index = f if fresh else sent_shard(link, step)
+        for link in used(plan, step, kind):
+            index = f if fresh else sent_shard(plan, link, step)
             pltpu.make_async_remote_copy(
                 src_ref=own(kind, lap) if fresh else place(kind, lap, index),
                 dst_ref=place(kind, lap, index),
@@ -144,14 +200,14 @@
 
     def gather_begin(lap):
         for kind in range(KINDS):
-            send(lap, 0, kind)
+            send(even, lap, 0, kind)
         for kind in range(KINDS):
             to_twin(lap, kind, f, own(kind, lap))
             keep_own(lap, kind).start()
 
-    def gather_step(lap, step, kind):
-        for link in range(LINKS):
-            target = place(kind, lap, got_shard(link, step))
+    def gather_step(plan, lap, step, kind, also=None):
+        for link in used(plan, step, kind):
+            target = place(kind, lap, got_shard(plan, link, step))
             pltpu.make_async_remote_copy(
                 src_ref=target,
                 dst_ref=target,
@@ -161,13 +217,40 @@
                 device_id_type=MESH,
             ).wait_recv()
         if isinstance(step, int):
-            if step + 1 < STEPS:
-                send(lap, step + 1, kind)
+            send(plan, lap, step + 1, kind)
         else:
-            pl.when(step + 1 < STEPS)(functools.partial(send, lap, step + 1, kind))
-        for link in range(LINKS):
-            index = got_shard(link, step)
+            pl.when(step + 1 < STEPS)(functools.partial(send, plan, lap, step + 1, kind))
+        if also is not None:
+            also()
+        for link in used(plan, step, kind):
+            index = got_shard(plan, link, step)
             to_twin(lap, kind, index, place(kind, lap, index))
+
+    def seat_of(stage, number, kind):
+        if kind < 2:
+            return passing.at[stage, number, kind]
+        return passing_second.at[stage, number]
+
+    def relay(stage, number, kind):
+        index = shard(0, -1 - number)
+        if stage == 0:
+            source, target, device = place(kind, 0, index), seat_of(0, number, kind), mate
+        elif stage == 1:
+            source, target, device = seat_of(0, number, kind), seat_of(1, number, kind), across
+        else:
+            source, target, device = seat_of(1, number, kind), place(kind, 0, index), mate
+        return pltpu.make_async_remote_copy(
+            src_ref=source,
+            dst_ref=target,
+            send_sem=relay_send.at[stage, number, kind],
+            recv_sem=relay_recv.at[stage, number, kind],
+            device_id=device,
+            device_id_type=MESH,
+        )
+
+    def pass_on(stage, number, kind):
+        relay(stage, number, kind).wait_recv()
+        relay(stage + 1, number, kind).start()
 
     def gather_end(lap, kind):
         whole = bulk(kind, lap, 16)
@@ -181,10 +264,10 @@
         ).wait_recv()
         keep_own(lap, kind).wait()
 
-    def gather_drain(lap):
+    def gather_drain(plan, lap):
         for kind in range(KINDS):
             for link in range(LINKS):
-                part = bulk(kind, lap, STEPS)
+                part = bulk(kind, lap, count(plan, link, kind))
                 pltpu.make_async_remote_copy(
                     src_ref=part,
                     dst_ref=part,
@@ -205,6 +288,12 @@
 
     gather_begin(0)
 
+    def columns(chunk):
+        return pl.ds(chunk * CW, CW)
+
+    base = jnp.where(core == 1, MOVED, 0)
+    groups = jnp.where(core == 1, MOST, GROUPS - MOVED)
+
     @pl.when(p == 0)
     def _():
         stage = pltpu.make_async_copy(inputs_ref, staged, stage_sem)
@@ -213,17 +302,84 @@
         for pair in range(MB // 2):
             even = staged[plan_ref[2 * pair]].astype(jnp.float32)
             odd = staged[plan_ref[2 * pair + 1]].astype(jnp.float32)
-            xbuf[0, 3 * pair] = even[:16].astype(jnp.bfloat16)
-            xbuf[0, 3 * pair + 1] = jnp.concatenate([even[16:], odd[:8]], axis=0).astype(
+            ordered[3 * pair] = even[:16].astype(jnp.bfloat16)
+            ordered[3 * pair + 1] = jnp.concatenate([even[16:], odd[:8]], axis=0).astype(
                 jnp.bfloat16
             )
-            xbuf[0, 3 * pair + 2] = odd[8:].astype(jnp.bfloat16)
-
-    for step in range(STEPS):
-        for kind in range(KINDS):
-            gather_step(0, step, kind)
-        if step == STEPS - 2:
-            gather_begin(1)
+            ordered[3 * pair + 2] = odd[8:].astype(jnp.bfloat16)
+
+    def fill(number, chunk):
+        return pltpu.make_async_copy(
+            ordered.at[number, :, columns(chunk)],
+            xbuf.at[0, base + number, :, columns(chunk)],
+            x_recv.at[0, base + number, chunk],
+        )
+
+    def over(number, chunk):
+        return pltpu.make_async_remote_copy(
+            src_ref=ordered.at[GROUPS - MOVED + number, :, columns(chunk)],
+            dst_ref=xbuf.at[0, number, :, columns(chunk)],
+            send_sem=over_send.at[number, chunk],
+            recv_sem=x_recv.at[0, number, chunk],
+            device_id=twin,
+            device_id_type=MESH,
+        )
+
+    def fill_all(number, carry):
+        for chunk in range(CHUNKS):
+            fill(number, chunk).start()
+        return carry
+
+    @pl.when(p == 0)
+    def _():
+        @pl.when(core == 0)
+        def _():
+            for number in range(MOVED):
+                for chunk in range(CHUNKS):
+                    over(number, chunk).start()
+
+        lax.fori_loop(0, jnp.where(core == 1, GROUPS, GROUPS - MOVED), fill_all, 0)
+
+    hurry = p < PIPE // 2
+
+    @pl.when(hurry)
+    def _():
+        for step in range(STEPS):
+            for kind in range(KINDS):
+                if step < RELAYED:
+                    gather_step(hurried, 0, step, kind, relay(0, step, kind).start)
+                else:
+                    gather_step(hurried, 0, step, kind)
+            if step == STEPS - 2:
+                gather_begin(1)
+        for number in range(RELAYED):
+            for kind in range(KINDS):
+                index = shard(1, -1 - number)
+                target = place(kind, 0, index)
+                pltpu.make_async_remote_copy(
+                    src_ref=target,
+                    dst_ref=target,
+                    send_sem=relay_send.at[2, number, kind],
+                    recv_sem=relay_recv.at[2, number, kind],
+                    device_id=mate,
+                    device_id_type=MESH,
+                ).wait_recv()
+                to_twin(0, kind, index, target)
+
+    @pl.when(jnp.logical_not(hurry))
+    def _():
+        last = len(patient[0])
+        for step in range(last):
+            for kind in range(KINDS):
+                for number in range(RELAYED):
+                    if step == number + 2:
+                        pass_on(1, number, kind)
+                    if step == number + 1:
+                        pass_on(0, number, kind)
+                gather_step(patient, 0, step, kind)
+            if step == last - 2:
+                gather_begin(1)
+
     for kind in range(KINDS - 1):
         gather_end(0, kind)
 
@@ -231,19 +387,15 @@
         for kind in range(KINDS):
             @pl.when(number % KINDS == kind)
             def _():
-                gather_step(1, number // KINDS, kind)
+                gather_step(even, 1, number // KINDS, kind)
 
         return carry
 
-    early = EARLY * p
+    early = EARLY * p - jnp.where(hurry, 0, LATER)
     lax.fori_loop(0, early, next_lap, 0)
 
     onward = ((p + 1) % PIPE, f)
-    turned = ((p + 1) % PIPE, shard(1, 0))
     crossing = (p % 4) == 3
-
-    def columns(chunk):
-        return pl.ds(chunk * CW, CW)
 
     def hop(lap, group, chunk, to_lap, device):
         return pltpu.make_async_remote_copy(
@@ -255,30 +407,40 @@
             device_id_type=MESH,
         )
 
-    def finish(group, second, slot):
+    def finish(group, number, second, slot, index):
+        if second:
+            seat = 0
+        else:
+            seat = jnp.where(number % 3 == 0, 0, 1)
         return pltpu.make_async_remote_copy(
             src_ref=xbuf.at[1, group],
-            dst_ref=landing.at[1 - second if second else jnp.where(group % 3 == 0, 0, 1)],
+            dst_ref=landing.at[seat],
             send_sem=end_send.at[second, group],
-            recv_sem=end_recv.at[1 - second if second else jnp.where(group % 3 == 0, 0, 1)],
-            device_id=(slot, f),
+            recv_sem=end_recv.at[seat],
+            device_id=(slot, index),
             device_id_type=MESH,
         )
 
-    def slots(group):
-        pair = group // 3
-        return 2 * pair + jnp.where(group % 3 == 2, 1, 0), 2 * pair + 1
+    def ends(group):
+        moved = (core == 1) & (group < MOVED)
+        number = jnp.where(moved, GROUPS - MOVED + group, group - base)
+        index = jnp.where(moved, other, f)
+        pair = number // 3
+        first = 2 * pair + jnp.where(number % 3 == 2, 1, 0)
+        leave = moved | (number < GROUPS - 1)
+        leave_too = (number % 3 == 1) & (moved | (number < GROUPS - 2))
+        return number, index, first, 2 * pair + 1, leave, leave_too
 
     def one(turn, carry):
-        lap = turn // GROUPS
-        group = turn % GROUPS
+        lap = jnp.where(turn >= groups, 1, 0)
+        group = turn - lap * groups
         step = early + turn - 1
 
-        @pl.when((turn > 0) & (turn < GROUPS) & (step < ROUNDS))
+        @pl.when((turn > 0) & (turn < groups) & (step < ROUNDS))
         def _():
             next_lap(step, 0)
 
-        @pl.when(turn == GROUPS)
+        @pl.when(turn == groups)
         def _():
             lax.fori_loop(jnp.minimum(step, ROUNDS), ROUNDS, next_lap, 0)
             for kind in range(KINDS):
@@ -288,10 +450,7 @@
         total_first = jnp.zeros((GROUP, H), jnp.float32)
         squares = jnp.zeros((GROUP, 1), jnp.float32)
         for chunk in range(CHUNKS):
-            @pl.when((p > 0) | (lap > 0))
-            def _():
-                hop(lap, group, chunk, lap, onward).wait_recv()
-
+            hop(lap, group, chunk, lap, onward).wait_recv()
             wide = xbuf[lap, group, :, columns(chunk)].astype(jnp.float32)
             squares += jnp.sum(wide * wide, axis=-1, keepdims=True)
             scaled = (wide * gains_ref[pl.ds(lap, 1), columns(chunk)]).astype(jnp.bfloat16)
@@ -311,35 +470,39 @@
 
         last = (p == PIPE - 1) & (lap == 1)
         to_lap = jnp.where(p == PIPE - 1, 1, lap)
-        turning = crossing & (lap == 0)
-        for chunk in range(CHUNKS):
+        target = (after, jnp.where(crossing & (lap == 0), shard(1, 0), f))
+
+        def down(chunk):
             wide = xbuf[lap, group, :, columns(chunk)].astype(jnp.float32)
             wide += jnp.dot(
                 hidden, w_second[lap, :, columns(chunk)], preferred_element_type=jnp.float32
             )
             xbuf[lap, group, :, columns(chunk)] = wide.astype(jnp.bfloat16)
 
-            @pl.when(jnp.logical_not(last | turning))
-            def _():
-                hop(lap, group, chunk, to_lap, onward).start()
-
-            @pl.when(turning)
-            def _():
-                hop(lap, group, chunk, to_lap, turned).start()
-
-        slot, after = slots(group)
-
-        @pl.when(last & (group < GROUPS - 1))
-        def _():
-            finish(group, 0, slot).start()
-
-        @pl.when(last & (group % 3 == 1) & (group < GROUPS - 2))
-        def _():
-            finish(group, 1, after).start()
+        @pl.when(jnp.logical_not(last))
+        def _():
+            for chunk in range(CHUNKS):
+                down(chunk)
+                hop(lap, group, chunk, to_lap, target).start()
+
+        @pl.when(last)
+        def _():
+            for chunk in range(CHUNKS):
+                down(chunk)
+
+        number, index, slot, next_slot, leave, leave_too = ends(group)
+
+        @pl.when(last & leave)
+        def _():
+            finish(group, number, 0, slot, index).start()
+
+        @pl.when(last & leave_too)
+        def _():
+            finish(group, number, 1, next_slot, index).start()
 
         return carry
 
-    lax.fori_loop(0, LAPS * GROUPS, one, 0)
+    lax.fori_loop(0, LAPS * groups, one, 0)
 
     def put(head, tail):
         head, tail = head.astype(jnp.float32), tail.astype(jnp.float32)
@@ -352,29 +515,51 @@
         def _():
             o_ref[0] = jnp.concatenate([head[8:], tail], axis=0).astype(jnp.bfloat16)
 
-    @pl.when(p < PIPE - 1)
-    def _():
-        for place_in in range(2):
+    at_hand = (p == PIPE - 1) & (core == 1)
+
+    @pl.when(jnp.logical_not(at_hand))
+    def _():
+        for seat in range(2):
             pltpu.make_async_remote_copy(
-                src_ref=landing.at[place_in],
-                dst_ref=landing.at[place_in],
+                src_ref=landing.at[seat],
+                dst_ref=landing.at[seat],
                 send_sem=end_send.at[0, 0],
-                recv_sem=end_recv.at[place_in],
+                recv_sem=end_recv.at[seat],
                 device_id=onward,
                 device_id_type=MESH,
             ).wait_recv()
         put(landing[0], landing[1])
 
-    @pl.when(p == PIPE - 1)
-    def _():
-        put(xbuf[1, GROUPS - 2], xbuf[1, GROUPS - 1])
-
-    for lap in range(LAPS):
-        gather_drain(lap)
+    @pl.when(at_hand)
+    def _():
+        put(xbuf[1, MOST - 2], xbuf[1, MOST - 1])
+
+    @pl.when((p == 0) & (core == 0))
+    def _():
+        for number in range(MOVED):
+            for chunk in range(CHUNKS):
+                over(number, chunk).wait_send()
+
+    @pl.when(hurry)
+    def _():
+        gather_drain(hurried, 0)
+        for number in range(RELAYED):
+            for kind in range(KINDS):
+                relay(0, number, kind).wait_send()
+
+    @pl.when(jnp.logical_not(hurry))
+    def _():
+        gather_drain(patient, 0)
+        for number in range(RELAYED):
+            for kind in range(KINDS):
+                relay(1, number, kind).wait_send()
+                relay(2, number, kind).wait_send()
+
+    gather_drain(even, 1)
 
     def sent(turn, carry):
-        lap = turn // GROUPS
-        group = turn % GROUPS
+        lap = jnp.where(turn >= groups, 1, 0)
+        group = turn - lap * groups
         last = (p == PIPE - 1) & (lap == 1)
 
         @pl.when(jnp.logical_not(last))
@@ -388,17 +573,19 @@
                 device_id_type=MESH,
             ).wait_send()
 
-        @pl.when(last & (group < GROUPS - 1))
-        def _():
-            finish(group, 0, 0).wait_send()
-
-        @pl.when(last & (group % 3 == 1) & (group < GROUPS - 2))
-        def _():
-            finish(group, 1, 0).wait_send()
+        number, index, slot, next_slot, leave, leave_too = ends(group)
+
+        @pl.when(last & leave)
+        def _():
+            finish(group, number, 0, slot, index).wait_send()
+
+        @pl.when(last & leave_too)
+        def _():
+            finish(group, number, 1, next_slot, index).wait_send()
 
         return carry
 
-    lax.fori_loop(0, LAPS * GROUPS, sent, 0)
+    lax.fori_loop(0, LAPS * groups, sent, 0)
 
 
 def local(inputs, gains, proj_gate, proj_in, proj_out, plan):
@@ -423,18 +610,24 @@
             pltpu.VMEM((LAPS, D, H), jnp.bfloat16),
             pltpu.VMEM((LAPS, H, D), jnp.bfloat16),
             pltpu.VMEM((MB, TOK, D), jnp.bfloat16),
-            pltpu.VMEM((LAPS, GROUPS, GROUP, D), jnp.bfloat16),
+            pltpu.VMEM((GROUPS, GROUP, D), jnp.bfloat16),
+            pltpu.VMEM((LAPS, MOST, GROUP, D), jnp.bfloat16),
             pltpu.VMEM((2, GROUP, D), jnp.bfloat16),
+            pltpu.VMEM((2, RELAYED, 2, SLICE, H), jnp.bfloat16),
+            pltpu.VMEM((2, RELAYED, H, SLICE), jnp.bfloat16),
             dma,
             dma((LAPS, KINDS)),
             dma((LAPS, LINKS, KINDS)),
-            dma((LAPS, LINKS, STEPS, KINDS)),
+            dma((LAPS, LINKS, STEPS + 1, KINDS)),
             dma((LAPS, KINDS)),
             dma((LAPS, KINDS)),
-            dma((LAPS, GROUPS)),
-            dma((LAPS, GROUPS, CHUNKS)),
-            dma((2, GROUPS)),
+            dma((LAPS, MOST)),
+            dma((LAPS, MOST, CHUNKS)),
+            dma((2, MOST)),
             dma((2,)),
+            dma((MOVED, CHUNKS)),
+            dma((3, RELAYED, KINDS)),
+            dma((3, RELAYED, KINDS)),
         ],
         compiler_params=pltpu.CompilerParams(
             collective_id=0, has_side_effects=True, vmem_limit_bytes=56 << 20

time: 180 us -> 176 us (0.978); the launches traced: 180 us -> 174 us
  Pallas kernels: 179 us -> 172 us
    pallas_call x1, Pallas kernels: 179 us -> 172 us  [local(): pl.pallas_call(kernel, out_shape=jax.ShapeDtypeStruct((1, TOK, D), jnp.bf...]
where the time goes in v3:
time: 176 us; the launch traced here: 174 us
  Pallas kernels  172 us (98%)
    pallas_call x1, Pallas kernels, local(): pl.pallas_call(kernel, out_shape=jax.ShapeDtypeStruct((1, TOK, D), jnp.bf...  172 us

profile of v3, /device:TPU:20, one launch (start us, length us, event | category | flops | bytes accessed | tf_op | source)
XLA Modules:
  0.0 174.1 jit_solution(5444570049880386805)
XLA Ops:
  0.0 172.4 %sections.1 = bf16[1,24,4096]{2,1,0:T(8,128)(2,1)} custom-call(s32[8]{0:T(128)} %plan_ref.1, bf16[8,24,4096]{2,1,0:T(8,128)(2,1)} %inputs_ref.1, f32[2,4096]{1,0:T(2,128)} %gains_ref.1, bf16[2,128,512]{2,1,0:T(8,128)(2,1)} %gate_ref.1, bf16[2,128,512]{2,1,0:T(8,128)(2,1)} %first_ref.1, bf16[2,512,128]{2,1,0:T(8,128)(2,1)} %second_ref.1), custom_call_target="tpu_custom_call" | custom-call | flops 4831838208 | bytes 25165824 | tf_op jit(solution)/shard_map/sections/pallas_call | solution.py:596
  172.5 1.6 copy.8

commit v4 on v3

--- a/solution.py
+++ b/solution.py
@@ -17,6 +17,8 @@
 MOST = GROUPS + MOVED
 CHUNKS = 8
 CW = D // CHUNKS
+WAITS = 4
+PER = CHUNKS // WAITS
 STEPS, LINKS, KINDS = 5, 3, 3
 ROUNDS = STEPS * KINDS
 EARLY = 2
@@ -288,8 +290,8 @@
 
     gather_begin(0)
 
-    def columns(chunk):
-        return pl.ds(chunk * CW, CW)
+    def columns(chunk, many=1):
+        return pl.ds(chunk * CW, many * CW)
 
     base = jnp.where(core == 1, MOVED, 0)
     groups = jnp.where(core == 1, MOST, GROUPS - MOVED)
@@ -312,7 +314,7 @@
         return pltpu.make_async_copy(
             ordered.at[number, :, columns(chunk)],
             xbuf.at[0, base + number, :, columns(chunk)],
-            x_recv.at[0, base + number, chunk],
+            x_recv.at[0, base + number, chunk // PER],
         )
 
     def over(number, chunk):
@@ -320,7 +322,7 @@
             src_ref=ordered.at[GROUPS - MOVED + number, :, columns(chunk)],
             dst_ref=xbuf.at[0, number, :, columns(chunk)],
             send_sem=over_send.at[number, chunk],
-            recv_sem=x_recv.at[0, number, chunk],
+            recv_sem=x_recv.at[0, number, chunk // PER],
             device_id=twin,
             device_id_type=MESH,
         )
@@ -330,17 +332,23 @@
             fill(number, chunk).start()
         return carry
 
-    @pl.when(p == 0)
-    def _():
-        @pl.when(core == 0)
-        def _():
-            for number in range(MOVED):
-                for chunk in range(CHUNKS):
-                    over(number, chunk).start()
-
-        lax.fori_loop(0, jnp.where(core == 1, GROUPS, GROUPS - MOVED), fill_all, 0)
-
     hurry = p < PIPE // 2
+
+    def fill_some(step):
+        part = GROUPS // 3
+        most = jnp.where(core == 1, GROUPS, GROUPS - MOVED)
+
+        @pl.when(p == 0)
+        def _():
+            if step == 0:
+
+                @pl.when(core == 0)
+                def _():
+                    for number in range(MOVED):
+                        for chunk in range(CHUNKS):
+                            over(number, chunk).start()
+
+            lax.fori_loop(step * part, jnp.minimum((step + 1) * part, most), fill_all, 0)
 
     @pl.when(hurry)
     def _():
@@ -350,6 +358,8 @@
                     gather_step(hurried, 0, step, kind, relay(0, step, kind).start)
                 else:
                     gather_step(hurried, 0, step, kind)
+            if step < 3:
+                fill_some(step)
             if step == STEPS - 2:
                 gather_begin(1)
         for number in range(RELAYED):
@@ -402,19 +412,20 @@
             src_ref=xbuf.at[lap, group, :, columns(chunk)],
             dst_ref=xbuf.at[to_lap, group, :, columns(chunk)],
             send_sem=x_send.at[lap, group],
-            recv_sem=x_recv.at[to_lap, group, chunk],
+            recv_sem=x_recv.at[to_lap, group, chunk // PER],
             device_id=device,
             device_id_type=MESH,
         )
 
-    def finish(group, number, second, slot, index):
+    def finish(group, number, second, slot, index, cut=None):
+        cut = pl.ds(0, D) if cut is None else cut
         if second:
             seat = 0
         else:
             seat = jnp.where(number % 3 == 0, 0, 1)
         return pltpu.make_async_remote_copy(
-            src_ref=xbuf.at[1, group],
-            dst_ref=landing.at[seat],
+            src_ref=xbuf.at[1, group, :, cut],
+            dst_ref=landing.at[seat, :, cut],
             send_sem=end_send.at[second, group],
             recv_sem=end_recv.at[seat],
             device_id=(slot, index),
@@ -449,16 +460,25 @@
         total_gate = jnp.zeros((GROUP, H), jnp.float32)
         total_first = jnp.zeros((GROUP, H), jnp.float32)
         squares = jnp.zeros((GROUP, 1), jnp.float32)
-        for chunk in range(CHUNKS):
-            hop(lap, group, chunk, lap, onward).wait_recv()
-            wide = xbuf[lap, group, :, columns(chunk)].astype(jnp.float32)
+        for part in range(WAITS):
+            wide_columns = columns(part * PER, PER)
+            arrived = xbuf.at[lap, group, :, wide_columns]
+            pltpu.make_async_remote_copy(
+                src_ref=arrived,
+                dst_ref=arrived,
+                send_sem=x_send.at[lap, group],
+                recv_sem=x_recv.at[lap, group, part],
+                device_id=onward,
+                device_id_type=MESH,
+            ).wait_recv()
+            wide = xbuf[lap, group, :, wide_columns].astype(jnp.float32)
             squares += jnp.sum(wide * wide, axis=-1, keepdims=True)
-            scaled = (wide * gains_ref[pl.ds(lap, 1), columns(chunk)]).astype(jnp.bfloat16)
+            scaled = (wide * gains_ref[pl.ds(lap, 1), wide_columns]).astype(jnp.bfloat16)
             total_gate += jnp.dot(
-                scaled, w_gate[lap, columns(chunk), :], preferred_element_type=jnp.float32
+                scaled, w_gate[lap, wide_columns, :], preferred_element_type=jnp.float32
             )
             total_first += jnp.dot(
-                scaled, w_first[lap, columns(chunk), :], preferred_element_type=jnp.float32
+                scaled, w_first[lap, wide_columns, :], preferred_element_type=jnp.float32
             )
         scale = lax.rsqrt(squares * (1.0 / D) + EPS)
         gate = total_gate * scale
@@ -487,18 +507,19 @@
 
         @pl.when(last)
         def _():
+            number, index, slot, next_slot, leave, leave_too = ends(group)
             for chunk in range(CHUNKS):
                 down(chunk)
-
-        number, index, slot, next_slot, leave, leave_too = ends(group)
-
-        @pl.when(last & leave)
-        def _():
-            finish(group, number, 0, slot, index).start()
-
-        @pl.when(last & leave_too)
-        def _():
-            finish(group, number, 1, next_slot, index).start()
+                if chunk % 2 == 1:
+                    cut = columns(chunk - 1, 2)
+
+                    @pl.when(leave)
+                    def _():
+                        finish(group, number, 0, slot, index, cut).start()
+
+                    @pl.when(leave_too)
+                    def _():
+                        finish(group, number, 1, next_slot, index, cut).start()
 
         return carry
 
@@ -622,7 +643,7 @@
             dma((LAPS, KINDS)),
             dma((LAPS, KINDS)),
             dma((LAPS, MOST)),
-            dma((LAPS, MOST, CHUNKS)),
+            dma((LAPS, MOST, WAITS)),
             dma((2, MOST)),
             dma((2,)),
             dma((MOVED, CHUNKS)),

time: 176 us -> 175 us (level)
  no operation moved by 1% of the time
where the time goes in v4:
time: 175 us; the launch traced here: 174 us
  Pallas kernels  173 us (99%)
    pallas_call x1, Pallas kernels, local(): pl.pallas_call(kernel, out_shape=jax.ShapeDtypeStruct((1, TOK, D), jnp.bf...  173 us

profile of v4, /device:TPU:20, one launch (start us, length us, event | category | flops | bytes accessed | tf_op | source)
XLA Modules:
  0.0 174.3 jit_solution(5222760408774912724)
XLA Ops:
  0.0 172.7 %sections.1 = bf16[1,24,4096]{2,1,0:T(8,128)(2,1)} custom-call(s32[8]{0:T(128)} %plan_ref.1, bf16[8,24,4096]{2,1,0:T(8,128)(2,1)} %inputs_ref.1, f32[2,4096]{1,0:T(2,128)} %gains_ref.1, bf16[2,128,512]{2,1,0:T(8,128)(2,1)} %gate_ref.1, bf16[2,128,512]{2,1,0:T(8,128)(2,1)} %first_ref.1, bf16[2,512,128]{2,1,0:T(8,128)(2,1)} %second_ref.1), custom_call_target="tpu_custom_call" | custom-call | flops 4831838208 | bytes 25165824 | tf_op jit(solution)/shard_map/sections/pallas_call | solution.py:617
  172.7 1.6 copy.8

commit v5 on v4

--- a/solution.py
+++ b/solution.py
@@ -19,6 +19,7 @@
 CW = D // CHUNKS
 WAITS = 4
 PER = CHUNKS // WAITS
+SENDS = ((0, 1), (1, 1), (2, 2), (4, 2), (6, 2))
 STEPS, LINKS, KINDS = 5, 3, 3
 ROUNDS = STEPS * KINDS
 EARLY = 2
@@ -407,10 +408,10 @@
     onward = ((p + 1) % PIPE, f)
     crossing = (p % 4) == 3
 
-    def hop(lap, group, chunk, to_lap, device):
+    def hop(lap, group, chunk, to_lap, device, many=1):
         return pltpu.make_async_remote_copy(
-            src_ref=xbuf.at[lap, group, :, columns(chunk)],
-            dst_ref=xbuf.at[to_lap, group, :, columns(chunk)],
+            src_ref=xbuf.at[lap, group, :, columns(chunk, many)],
+            dst_ref=xbuf.at[to_lap, group, :, columns(chunk, many)],
             send_sem=x_send.at[lap, group],
             recv_sem=x_recv.at[to_lap, group, chunk // PER],
             device_id=device,
@@ -492,18 +493,18 @@
         to_lap = jnp.where(p == PIPE - 1, 1, lap)
         target = (after, jnp.where(crossing & (lap == 0), shard(1, 0), f))
 
-        def down(chunk):
-            wide = xbuf[lap, group, :, columns(chunk)].astype(jnp.float32)
+        def down(chunk, many=1):
+            wide = xbuf[lap, group, :, columns(chunk, many)].astype(jnp.float32)
             wide += jnp.dot(
-                hidden, w_second[lap, :, columns(chunk)], preferred_element_type=jnp.float32
+                hidden, w_second[lap, :, columns(chunk, many)], preferred_element_type=jnp.float32
             )
-            xbuf[lap, group, :, columns(chunk)] = wide.astype(jnp.bfloat16)
+            xbuf[lap, group, :, columns(chunk, many)] = wide.astype(jnp.bfloat16)
 
         @pl.when(jnp.logical_not(last))
         def _():
-            for chunk in range(CHUNKS):
-                down(chunk)
-                hop(lap, group, chunk, to_lap, target).start()
+            for chunk, many in SENDS:
+                down(chunk, many)
+                hop(lap, group, chunk, to_lap, target, many).start()
 
         @pl.when(last)
         def _():

time: 175 us -> 177 us (1.011)
  Pallas kernels: 173 us -> 175 us
    pallas_call x1, Pallas kernels: 173 us -> 175 us  [local(): pl.pallas_call(kernel, out_shape=jax.ShapeDtypeStruct((1, TOK, D), jnp.bf...]
where the time goes in v5:
time: 177 us; the launch traced here: 176 us
  Pallas kernels  175 us (99%)
    pallas_call x1, Pallas kernels, local(): pl.pallas_call(kernel, out_shape=jax.ShapeDtypeStruct((1, TOK, D), jnp.bf...  175 us

profile of v5, /device:TPU:20, one launch (start us, length us, event | category | flops | bytes accessed | tf_op | source)
XLA Modules:
  0.0 176.4 jit_solution(17772156721131097862)
XLA Ops:
  0.0 174.8 %sections.1 = bf16[1,24,4096]{2,1,0:T(8,128)(2,1)} custom-call(s32[8]{0:T(128)} %plan_ref.1, bf16[8,24,4096]{2,1,0:T(8,128)(2,1)} %inputs_ref.1, f32[2,4096]{1,0:T(2,128)} %gains_ref.1, bf16[2,128,512]{2,1,0:T(8,128)(2,1)} %gate_ref.1, bf16[2,128,512]{2,1,0:T(8,128)(2,1)} %first_ref.1, bf16[2,512,128]{2,1,0:T(8,128)(2,1)} %second_ref.1), custom_call_target="tpu_custom_call" | custom-call | flops 4831838208 | bytes 25165824 | tf_op jit(solution)/shard_map/sections/pallas_call | solution.py:618
  174.8 1.6 copy.8
